TPU v7x, 32 devices: a whole 2x2x4 slice. The times are simulated.
32 devices in a mesh: fsdp: 4 (over z), ctx: 4 (over x, core), tp: 2 (over y).
Axes of the slice: x: 2, y: 2, z: 4, core: 2. Of those that a mesh axis runs over, the one named last changes fastest.
Arguments:
- hidden_in: bfloat16 [4096, 2048], P(('fsdp', 'ctx')), may hold values from -6 to 6
- cotangent: bfloat16 [4096, 2048], P(('fsdp', 'ctx')), may hold values from -6 to 6
- routes: int32 [4096, 6], P(('fsdp', 'ctx')), may hold values from 0 to 15, all different within a row; in each aligned block of 256 rows (0 to 255, 256 to 511, ...) at most 128 rows name the same one
- gate_weights: float32 [4096, 6], P(('fsdp', 'ctx')), may hold values from 0.05 to 0.35
- gain_attn: bfloat16 [2048], P('fsdp'), may hold values from 0.5 to 1.5
- gain_latent: bfloat16 [512], P('fsdp'), may hold values from 0.5 to 1.5
- w_query: bfloat16 [2048, 3072], P('fsdp', 'tp'), may hold values from -0.1875 to 0.1875
- w_latent: bfloat16 [2048, 576], P('fsdp'), may hold values from -0.125 to 0.125
- w_expand: bfloat16 [512, 4096], P('fsdp', 'tp'), may hold values from -0.25 to 0.25
- w_out: bfloat16 [2048, 2048], P('tp', 'fsdp'), may hold values from -1.5 to 1.5
- gain_moe: bfloat16 [2048], P('fsdp'), may hold values from 0.5 to 1.5
- expert_gate: bfloat16 [16, 2048, 1408], P(None, 'fsdp', 'tp'), may hold values from -0.125 to 0.125
- expert_up: bfloat16 [16, 2048, 1408], P(None, 'fsdp', 'tp'), may hold values from -0.125 to 0.125
- expert_down: bfloat16 [16, 1408, 2048], P(None, 'tp', 'fsdp'), may hold values from -0.4375 to 0.4375
- shared_gate: bfloat16 [2048, 2816], P('fsdp', 'tp'), may hold values from -0.125 to 0.125
- shared_up: bfloat16 [2048, 2816], P('fsdp', 'tp'), may hold values from -0.125 to 0.125
- shared_down: bfloat16 [2816, 2048], P('tp', 'fsdp'), may hold values from -0.15625 to 0.15625
Outputs:
- layer_out: bfloat16 [4096, 2048], P(('fsdp', 'ctx'))
- input_grad: float32 [4096, 2048], P(('fsdp', 'ctx'))
- gates_grad: float32 [4096, 6], P(('fsdp', 'ctx'))
- gain_attn_grad: float32 [2048], P('fsdp')
- gain_latent_grad: float32 [512], P('fsdp')
- w_query_grad: float32 [2048, 3072], P('fsdp', 'tp')
- w_latent_grad: float32 [2048, 576], P('fsdp')
- w_expand_grad: float32 [512, 4096], P('fsdp', 'tp')
- w_out_grad: float32 [2048, 2048], P('tp', 'fsdp')
- gain_moe_grad: float32 [2048], P('fsdp')
- expert_gate_grad: float32 [16, 2048, 1408], P(None, 'fsdp', 'tp')
- expert_up_grad: float32 [16, 2048, 1408], P(None, 'fsdp', 'tp')
- expert_down_grad: float32 [16, 1408, 2048], P(None, 'tp', 'fsdp')
- shared_gate_grad: float32 [2048, 2816], P('fsdp', 'tp')
- shared_up_grad: float32 [2048, 2816], P('fsdp', 'tp')
- shared_down_grad: float32 [2816, 2048], P('tp', 'fsdp')
Inputs may be any that keep to these rules, and one draw needn't show every extreme that they name: `routes`: each row names 6 different experts; in each aligned block of 256 rows (the rows of one device) no expert is named by more than 128 rows, a bound that some block reaches.
All inputs are finite; a program needn't handle non-finite values.
Results may differ from a plain program's by a relative error of at most 0.025.
Values may be sent and summed in bfloat16 or wider, within the bound.
No kernel may reach another device: no remote copies, remote signals or barrier semaphores. Data moves between devices by JAX's collectives and lax.ppermute only.
A program may use at most 512 MiB of HBM per device.

v0:
```python
import math

import jax
import jax.numpy as jnp
from jax import lax
from jax.experimental import pallas as pl
from jax.experimental.pallas import tpu as pltpu
from jax.sharding import PartitionSpec as P

NOPE = 128
ROPE = 64
LATENT = 512
VHEAD = 128
EXPERTS = 16
TOPK = 6
CAPACITY = 128
EPSILON = 1e-06

f32 = jnp.float32
bf16 = jnp.bfloat16


def norm_rows(values, gain_vec):
    scales = lax.rsqrt(jnp.mean(values * values, axis=-1, keepdims=True) + EPSILON)
    return (values * scales * gain_vec, scales)


def norm_back(values, scales, gain_vec, gradient):
    weighted = gradient * gain_vec
    inner = jnp.mean(weighted * values, axis=-1, keepdims=True)
    return (
        scales * weighted - values * scales**3 * inner,
        jnp.sum(gradient * values * scales, axis=0),
    )


def angle_tables(position, width):
    half_width = width // 2
    frequency = jnp.exp(
        jnp.arange(half_width, dtype=f32) * (-2.0 * math.log(10000.0) / width)
    )
    angles = position.astype(f32)[:, None] * frequency[None, :]
    return (jnp.cos(angles), jnp.sin(angles))


def rotate(values, cosine, sine_tab):
    half_width = values.shape[-1] // 2
    front_half = values[..., :half_width]
    back_half = values[..., half_width:]
    return jnp.concatenate(
        [front_half * cosine - back_half * sine_tab, back_half * cosine + front_half * sine_tab],
        axis=-1,
    )


def rotate_back(gradient, cosine, sine_tab):
    return rotate(gradient, cosine, -sine_tab)


def swiglu_back(gate_act, up_act, grad_hidden):
    sigmoid_g = jax.nn.sigmoid(gate_act)
    grad_up = (grad_hidden * gate_act * sigmoid_g).astype(bf16)
    grad_gate = (grad_hidden * up_act * sigmoid_g * (1.0 + gate_act * (1.0 - sigmoid_g))).astype(
        bf16
    )
    return (grad_gate, grad_up)


def mm(left, right):
    return jnp.dot(left, right, preferred_element_type=f32)


def mm_nt(left, right):
    return lax.dot_general(left, right, (((1,), (1,)), ((), ())), preferred_element_type=f32)


def mm_tn(left, right):
    return lax.dot_general(left, right, (((0,), (0,)), ((), ())), preferred_element_type=f32)


def after(value, *earlier):
    return lax.optimization_barrier((value,) + earlier)[0]


def exchange(value, axis, bit):
    size = lax.axis_size(axis)
    return lax.ppermute(value, axis, [(a, a ^ bit) for a in range(size)])


def high_bits(size):
    bit = size // 2
    while bit >= 2:
        yield bit
        bit //= 2


def low_bits(size):
    bit = 1
    while bit < size:
        yield bit
        bit *= 2


def place(shape, dtype, parts, starts, axis):
    buffer = jnp.zeros(shape, dtype)
    for part, start in zip(parts, starts):
        buffer = lax.dynamic_update_slice_in_dim(buffer, part.astype(dtype), start, axis)
    return buffer


def slot_masks(row_ref, pieces, tokens):
    iota = lax.broadcasted_iota(jnp.int32, (CAPACITY, tokens), 0)
    return [iota == row_ref[a] for a in range(pieces)]


def one_hot(mask):
    return jnp.where(mask, 1.0, 0.0).astype(bf16)


def rows_kernel(pieces, fs, steps, groups, *refs):
    row_ref, ws_ref = refs[:2]
    xs, dys = refs[2 : 2 + 2 * groups], refs[2 + 2 * groups : 2 + 4 * groups]
    wg, wu = refs[2 + 4 * groups : 4 + 4 * groups]
    slots_ref, sdy_ref, gate_ref, up_ref, ds_ref, dsh_ref, xbuf, dybuf, sems = refs[
        4 + 4 * groups :
    ]
    ffn = gate_ref.shape[1]
    step = pl.program_id(0)
    slot = lax.rem(step, 2)
    width = xbuf.shape[4]
    tokens = xbuf.shape[2] * xbuf.shape[3]
    dpart = wg.shape[2]
    shp = ws_ref.shape[0] // 3
    per = steps // (2 * groups)

    def begin(at, into):
        for q in range(steps):

            @pl.when(at == q)
            def _(q=q):
                chunk, other = q // 2, q % 2
                which, c = 2 * (chunk // per) + other, chunk % per
                pltpu.make_async_copy(xs[which].at[:, :, c], xbuf.at[into], sems.at[into, 0]).start()
                pltpu.make_async_copy(
                    dys[which].at[:, :, c], dybuf.at[into], sems.at[into, 1]
                ).start()

    @pl.when(step == 0)
    def _():
        begin(step, 0)

    @pl.when(step + 1 < steps)
    def _():
        begin(step + 1, 1 - slot)

    pltpu.make_async_copy(xs[0].at[:, :, 0], xbuf.at[slot], sems.at[slot, 0]).wait()
    pltpu.make_async_copy(dys[0].at[:, :, 0], dybuf.at[slot], sems.at[slot, 1]).wait()
    masks = slot_masks(row_ref, pieces, tokens)
    for a in range(pieces):
        pick = one_hot(masks[a])
        of = slice(a * CAPACITY, (a + 1) * CAPACITY)
        slots_ref[of, :] = mm(pick, xbuf[slot, a].reshape(tokens, width)).astype(bf16)
        sdy_ref[of, :] = mm(pick, dybuf[slot, a].reshape(tokens, width)).astype(bf16)
    gate_act = up_act = None
    for s in range(fs):
        part = slots_ref[:, s * dpart : (s + 1) * dpart]
        g, u = mm_nt(part, wg[s]), mm_nt(part, wu[s])
        gate_act = g if s == 0 else gate_act + g
        up_act = u if s == 0 else up_act + u
    gate_ref[...] = gate_act
    up_ref[...] = up_act
    flat = xbuf[slot].reshape(pieces * tokens, width)
    dflat = dybuf[slot].reshape(pieces * tokens, width)
    both = mm_nt(flat, ws_ref[: 2 * shp])
    sg, su = both[:, :shp], both[:, shp:]
    sd = mm_nt(dflat, ws_ref[2 * shp :])
    sig = 1.0 / (1.0 + jnp.exp(-sg))
    silu = sg * sig
    s_hid = (silu * su).astype(bf16)
    ds_up = (sd * silu).astype(bf16)
    ds_gate = (sd * su * sig * (1.0 + sg * (1.0 - sig))).astype(bf16)
    ds_ref[:, :shp] = ds_gate
    ds_ref[:, shp : 2 * shp] = ds_up
    ds_ref[:, 2 * shp :] = s_hid
    first = mm_tn(ds_ref[:, : 2 * shp], flat)
    second = mm_tn(s_hid, dflat)

    @pl.when(step == 0)
    def _():
        dsh_ref[: 2 * shp] = first
        dsh_ref[2 * shp :] = second

    @pl.when(step > 0)
    def _():
        dsh_ref[: 2 * shp] += first
        dsh_ref[2 * shp :] += second


def moe_rows(fs, ffn, xs, dys, slot_row, shared, gate_w, up_w):
    pieces, tp, per, n, width = xs[0].shape
    groups = len(xs) // 2
    tokens = tp * n
    steps = 2 * groups * per
    shp = shared.shape[0] // 3
    slots = pieces * CAPACITY
    once = pl.Buffered(buffer_count=1)

    def by_step(shape):
        return pl.BlockSpec(shape, lambda q: (q,) + (0,) * (len(shape) - 1))

    def fixed(shape):
        return pl.BlockSpec(shape, lambda q: (0,) * len(shape), pipeline_mode=once)

    total = steps * slots
    return pl.pallas_call(
        lambda *refs: rows_kernel(pieces, fs, steps, groups, *refs),
        grid=(steps,),
        in_specs=[by_step((pieces, 1, tokens)), fixed((3 * shp, width))]
        + [pl.BlockSpec(memory_space=pl.ANY)] * (4 * groups)
        + [fixed(gate_w.shape), fixed(up_w.shape)],
        out_specs=[
            by_step((slots, width)),
            by_step((slots, width)),
            by_step((slots, ffn)),
            by_step((slots, ffn)),
            by_step((pieces * tokens, 3 * shp)),
            fixed((3 * shp, width)),
        ],
        scratch_shapes=[
            pltpu.VMEM((2, pieces, tp, n, width), bf16),
            pltpu.VMEM((2, pieces, tp, n, width), bf16),
            pltpu.SemaphoreType.DMA((2, 2)),
        ],
        out_shape=[
            jax.ShapeDtypeStruct((total, width), bf16),
            jax.ShapeDtypeStruct((total, width), bf16),
            jax.ShapeDtypeStruct((total, ffn), f32),
            jax.ShapeDtypeStruct((total, ffn), f32),
            jax.ShapeDtypeStruct((steps * pieces * tokens, 3 * shp), bf16),
            jax.ShapeDtypeStruct((3 * shp, width), f32),
        ],
        compiler_params=pltpu.CompilerParams(vmem_limit_bytes=60 * 1024 * 1024),
        cost_estimate=pl.CostEstimate(flops=0, bytes_accessed=1_000_000, transcendentals=0),
        name="moe_rows",
    )(slot_row, shared, *xs, *dys, gate_w, up_w)


def back_kernel(pieces, fs, extra, tp_first, me_ref, *refs):
    sdy_ref, gate_ref, up_ref, row_ref, col_ref, wt_ref, ds_ref, ws_ref, wg, wu, wd = refs[:11]
    name_ref = refs[11]
    dg_ref, du_ref, hw_ref, keep_ref, send_ref = refs[12 + extra :]
    ffn = gate_ref.shape[1]
    n, width = keep_ref.shape[3], ws_ref.shape[1]
    half = lax.rem(pl.program_id(0), 2)
    tokens = row_ref.shape[2]
    dpart = wg.shape[2]
    shp = ws_ref.shape[0] // 3
    masks = slot_masks(row_ref, pieces, tokens)
    weight = jnp.concatenate(
        [
            jnp.sum(jnp.where(masks[a], wt_ref[a], 0.0), axis=1, keepdims=True)
            for a in range(pieces)
        ],
        axis=0,
    )
    dy_down = None
    for s in range(fs):
        d = mm_nt(sdy_ref[:, s * dpart : (s + 1) * dpart], wd[s])
        dy_down = d if s == 0 else dy_down + d
    gate_act, up_act = gate_ref[...], up_ref[...]
    sig = 1.0 / (1.0 + jnp.exp(-gate_act))
    silu = gate_act * sig
    hidden = (silu * up_act).astype(bf16).astype(f32)
    slot_grad = jnp.sum(hidden * dy_down, axis=1, keepdims=True)
    hw_ref[...] = (weight * hidden).astype(bf16)
    d_hidden = weight * dy_down
    du_ref[...] = (d_hidden * silu).astype(bf16)
    dg_ref[...] = (d_hidden * up_act * sig * (1.0 + gate_act * (1.0 - sig))).astype(bf16)
    across = lax.broadcasted_iota(jnp.int32, (tokens, CAPACITY), 1)
    picks = [one_hot(across == col_ref[a]) for a in range(pieces)]

    def write(a, at, value):
        for t in range(tokens // n):
            rows = value[t * n : (t + 1) * n]
            at_t = me_ref[0] ^ t
            index = (at_t, a) if tp_first else (a, at_t)

            @pl.when(half == 0)
            def _():
                keep_ref[index[0], index[1], 0, :, at] = rows

            @pl.when(half == 1)
            def _():
                send_ref[index[0], index[1], 0, :, at] = rows

    for s in range(fs):
        at = slice(s * dpart, (s + 1) * dpart)
        back = (
            mm(dg_ref[...], wg[s]) + mm(du_ref[...], wu[s])
        ).astype(bf16)
        s_back = mm(ds_ref[:, : 2 * shp], ws_ref[: 2 * shp, at])
        for a in range(pieces):
            part = mm(picks[a], back[a * CAPACITY : (a + 1) * CAPACITY])
            write(a, at, (part + s_back[a * tokens : (a + 1) * tokens]).astype(bf16))
    spread = (slot_grad * name_ref[...]).astype(bf16)
    for a in range(pieces):
        part = mm(picks[a], spread[a * CAPACITY : (a + 1) * CAPACITY])
        write(a, slice(width, width + 128), part.astype(bf16))


def moe_back(
    first, chunks, tp, fs, tp_first, me, sdy, gate, up, slot_row, slot_col, weight, ds, shared, gate_w, up_w, down_w, name, big
):
    width = sdy.shape[1]
    all_pieces, _, tokens = slot_row.shape
    pieces = all_pieces // (2 * fs)
    ffn, dpart = down_w.shape[1:]
    shp = shared.shape[0] // 3
    slots = pieces * CAPACITY
    once = pl.Buffered(buffer_count=1)

    def by_step(shape):
        return pl.BlockSpec(shape, lambda q, me: (2 * first + q,) + (0,) * (len(shape) - 1))

    def fixed(shape):
        return pl.BlockSpec(shape, lambda q, me: (0,) * len(shape), pipeline_mode=once)

    n = tokens // tp
    outer = (tp, pieces) if tp_first else (pieces, tp)
    half_spec = pl.BlockSpec(outer + (1, n, width + 128), lambda q, me: (0, 0, q // 2, 0, 0))
    total = sdy.shape[0]
    half = jax.ShapeDtypeStruct(outer + (chunks, n, width + 128), bf16)
    return pl.pallas_call(
        lambda *refs: back_kernel(pieces, fs, len(big), tp_first, *refs),
        grid_spec=pltpu.PrefetchScalarGridSpec(
            num_scalar_prefetch=1,
            grid=(2 * chunks,),
            in_specs=[
                by_step((slots, width)),
                by_step((slots, ffn)),
                by_step((slots, ffn)),
                by_step((pieces, 1, tokens)),
                by_step((pieces, tokens, 1)),
                by_step((pieces, 1, tokens)),
                by_step((pieces * tokens, 3 * shp)),
                fixed((3 * shp, width)),
            ]
            + [fixed(gate_w.shape), fixed(up_w.shape), fixed((fs, ffn, dpart))]
            + [fixed((1, 128))]
            + [pl.BlockSpec(memory_space=pl.ANY)] * len(big),
            out_specs=[
                by_step((slots, ffn)),
                by_step((slots, ffn)),
                by_step((slots, ffn)),
                half_spec,
                half_spec,
            ],
        ),
        out_shape=[
            jax.ShapeDtypeStruct((total, ffn), bf16),
            jax.ShapeDtypeStruct((total, ffn), bf16),
            jax.ShapeDtypeStruct((total, ffn), bf16),
            half,
            half,
        ],
        input_output_aliases={13 + b: b for b in range(len(big))},
        compiler_params=pltpu.CompilerParams(vmem_limit_bytes=60 * 1024 * 1024),
        cost_estimate=pl.CostEstimate(flops=0, bytes_accessed=1_000_000, transcendentals=0),
        name="moe_back",
    )(me, sdy, gate, up, slot_row, slot_col, weight, ds, shared, gate_w, up_w, down_w, name, *big)


def out_kernel(pieces, fs, ctx_first, me_ref, hw_ref, col_ref, ds_ref, ws_ref, wd, keep_ref, send_ref):
    tokens = col_ref.shape[1]
    n = keep_ref.shape[3]
    half = lax.rem(pl.program_id(0), 2)
    dpart = wd.shape[2]
    across = lax.broadcasted_iota(jnp.int32, (tokens, CAPACITY), 1)
    picks = [one_hot(across == col_ref[a]) for a in range(pieces)]
    for s in range(fs):
        at = slice(s * dpart, (s + 1) * dpart)
        out = mm(hw_ref[...], wd[s]).astype(bf16)
        shared = mm(ds_ref[...], ws_ref[:, at])
        for a in range(pieces):
            part = mm(picks[a], out[a * CAPACITY : (a + 1) * CAPACITY])
            value = (part + shared[a * tokens : (a + 1) * tokens]).astype(bf16)
            for t in range(tokens // n):
                rows = value[t * n : (t + 1) * n]
                at_t = me_ref[0] ^ t
                index = (a, at_t) if ctx_first else (at_t, a)

                @pl.when(half == 0)
                def _():
                    keep_ref[index[0], index[1], 0, :, at] = rows

                @pl.when(half == 1)
                def _():
                    send_ref[index[0], index[1], 0, :, at] = rows


def moe_out(first, chunks, tp, fs, ctx_first, me, hw, slot_col, ds, shared, down_w):
    all_pieces, tokens, _ = slot_col.shape
    ffn, dpart = down_w.shape[1:]
    width = shared.shape[1]
    shp = shared.shape[0] // 3
    pieces = all_pieces // (2 * fs)
    n = tokens // tp
    once = pl.Buffered(buffer_count=1)
    slots = 2 * chunks * pieces * CAPACITY
    outer = (pieces, tp) if ctx_first else (tp, pieces)
    half_spec = pl.BlockSpec(outer + (1, n, width), lambda q, me: (0, 0, q // 2, 0, 0))
    return pl.pallas_call(
        lambda *refs: out_kernel(pieces, fs, ctx_first, *refs),
        grid_spec=pltpu.PrefetchScalarGridSpec(
            num_scalar_prefetch=1,
            grid=(2 * chunks,),
            in_specs=[
                pl.BlockSpec((pieces * CAPACITY, ffn), lambda q, me: (2 * first + q, 0)),
                pl.BlockSpec((pieces, tokens, 1), lambda q, me: (2 * first + q, 0, 0)),
                pl.BlockSpec((pieces * tokens, shp), lambda q, me: (2 * first + q, 2)),
                pl.BlockSpec((shp, width), lambda q, me: (2, 0), pipeline_mode=once),
                pl.BlockSpec((fs, ffn, dpart), lambda q, me: (0, 0, 0), pipeline_mode=once),
            ],
            out_specs=[half_spec, half_spec],
        ),
        out_shape=[jax.ShapeDtypeStruct(outer + (chunks, n, width), bf16)] * 2,
        compiler_params=pltpu.CompilerParams(vmem_limit_bytes=40 * 1024 * 1024),
        cost_estimate=pl.CostEstimate(flops=0, bytes_accessed=1_000_000, transcendentals=0),
        name="moe_out",
    )(me, hw, slot_col, ds, shared, down_w)


def turned(front, back, cosine, sine):
    return front * cosine - back * sine, back * cosine + front * sine


def attend_kernel(hd, normed, query, latent, expand, out_w, gain, cos, sin, posq, posk, *outs):
    keep_ref, send_ref, raw_ref, low_ref, q_ref, ex_ref, prob_ref, heads_ref = outs
    length = normed.shape[0]
    q_width, kv_width, turn = NOPE + ROPE, NOPE + VHEAD, ROPE // 2
    scaling = q_width ** (-0.5)
    q_raw = mm_nt(normed[...], query[...])
    for h in range(hd):
        at = h * q_width
        q_ref[:, at : at + NOPE] = q_raw[:, at : at + NOPE].astype(bf16)
        front, back = q_raw[:, at + NOPE : at + NOPE + turn], q_raw[:, at + NOPE + turn : at + q_width]
        front, back = turned(front, back, cos[...], sin[...])
        q_ref[:, at + NOPE : at + NOPE + turn] = front.astype(bf16)
        q_ref[:, at + NOPE + turn : at + q_width] = back.astype(bf16)
    raw = mm_nt(normed[...], latent[...])
    raw_ref[...] = raw
    body = raw[:, :LATENT]
    scales = lax.rsqrt(jnp.mean(body * body, axis=-1, keepdims=True) + EPSILON)
    low_ref[:, :LATENT] = (body * scales * gain[...]).astype(bf16)
    front, back = turned(raw[:, LATENT : LATENT + turn], raw[:, LATENT + turn :], cos[...], sin[...])
    low_ref[:, LATENT : LATENT + turn] = front.astype(bf16)
    low_ref[:, LATENT + turn :] = back.astype(bf16)
    ex_ref[...] = mm(low_ref[:, :LATENT], expand[...]).astype(bf16)
    rope = low_ref[:, LATENT:]
    block = min(256, length)
    for h in range(hd):
        at, kv = h * q_width, h * kv_width
        keys, vals = ex_ref[:, kv : kv + NOPE], ex_ref[:, kv + NOPE : kv + kv_width]
        for r in range(0, length, block):
            rows = slice(r, r + block)
            scores = mm_nt(q_ref[rows, at : at + NOPE], keys)
            scores = (scores + mm_nt(q_ref[rows, at + NOPE : at + q_width], rope)) * scaling
            scores = jnp.where(posk[...] <= posq[rows, :], scores, -1e30)
            exponent = jnp.exp(scores - jnp.max(scores, axis=-1, keepdims=True))
            total = jnp.sum(exponent, axis=-1, keepdims=True)
            prob = (exponent / total).astype(bf16)
            prob_ref[h, rows, :] = prob
            heads_ref[rows, h * VHEAD : (h + 1) * VHEAD] = mm(prob, vals).astype(bf16)
    tp, pairs, n, _ = keep_ref.shape
    for ref, start in ((send_ref, length // 2), (keep_ref, 0)):
        for p in range(pairs):
            for t in range(tp):
                at = start + (p * tp + t) * n
                ref[t, p] = mm(heads_ref[at : at + n], out_w[...]).astype(bf16)


def whole_call(body, operands, out_shape, name, declared=1_000_000):
    return pl.pallas_call(
        body,
        in_specs=[pl.BlockSpec(memory_space=pltpu.VMEM)] * len(operands),
        out_specs=[pl.BlockSpec(memory_space=pltpu.VMEM)] * len(out_shape),
        out_shape=[jax.ShapeDtypeStruct(shape, dtype) for shape, dtype in out_shape],
        compiler_params=pltpu.CompilerParams(vmem_limit_bytes=60 * 1024 * 1024),
        cost_estimate=pl.CostEstimate(flops=0, bytes_accessed=declared, transcendentals=0),
        name=name,
    )(*operands)


def attend(hd, lead, normed, query, latent, expand, out_w, gain, cos, sin, position):
    length, width = normed.shape
    operands = (
        normed,
        query,
        latent,
        expand,
        out_w,
        gain[None],
        cos,
        sin,
        position[:, None],
        position[None],
    )
    out_shape = [
        (lead + (width,), bf16),
        (lead + (width,), bf16),
        ((length, LATENT + ROPE), f32),
        ((length, LATENT + ROPE), bf16),
        ((length, hd * (NOPE + ROPE)), bf16),
        ((length, hd * (NOPE + VHEAD)), bf16),
        ((hd, length, length), bf16),
        ((length, hd * VHEAD), bf16),
    ]
    return whole_call(lambda *refs: attend_kernel(hd, *refs), operands, out_shape, "attend")


def attend_back_kernel(hd, grad, out_w, prob, heads, ex, low, q, cos, sin, query, expand, *outs):
    keep_ref, send_ref, dq_ref, dex_ref = outs
    length, width = grad.shape
    half = length // 2
    q_width, kv_width, turn = NOPE + ROPE, NOPE + VHEAD, ROPE // 2
    scaling = q_width ** (-0.5)
    d_heads = mm_nt(grad[...], out_w[...]).astype(bf16)
    rope = low[:, LATENT:]
    block = min(256, length)
    d_rope = None
    for h in range(hd):
        at, kv = h * q_width, h * kv_width
        of = slice(h * VHEAD, (h + 1) * VHEAD)
        keys, vals = ex[:, kv : kv + NOPE], ex[:, kv + NOPE : kv + kv_width]
        d_key = d_kr = d_val = None
        for r in range(0, length, block):
            rows = slice(r, r + block)
            d_out = d_heads[rows, of]
            inner = jnp.sum(
                d_out.astype(f32) * heads[rows, of].astype(f32), axis=-1, keepdims=True
            )
            p = prob[h, rows, :]
            d_scores = (p.astype(f32) * (mm_nt(d_out, vals) - inner)).astype(bf16)
            dq_ref[rows, at : at + NOPE] = (mm(d_scores, keys) * scaling).astype(bf16)
            d_turn = mm(d_scores, rope) * scaling
            front, back = turned(d_turn[:, :turn], d_turn[:, turn:], cos[rows, :], -sin[rows, :])
            dq_ref[rows, at + NOPE : at + NOPE + turn] = front.astype(bf16)
            dq_ref[rows, at + NOPE + turn : at + q_width] = back.astype(bf16)
            one = mm_tn(d_scores, q[rows, at : at + NOPE])
            two = mm_tn(d_scores, q[rows, at + NOPE : at + q_width])
            three = mm_tn(p, d_out)
            d_key = one if r == 0 else d_key + one
            d_kr = two if r == 0 else d_kr + two
            d_val = three if r == 0 else d_val + three
        dex_ref[:, kv : kv + NOPE] = (d_key * scaling).astype(bf16)
        dex_ref[:, kv + NOPE : kv + kv_width] = d_val.astype(bf16)
        d_rope = d_kr if h == 0 else d_rope + d_kr
    d_rope = (d_rope * scaling).astype(bf16)
    tp, pairs, n, _ = keep_ref.shape
    for ref, start in ((send_ref, half), (keep_ref, 0)):
        for p in range(pairs):
            for t in range(tp):
                at = start + (p * tp + t) * n
                rows = slice(at, at + n)
                ref[t, p, :, :width] = mm(dq_ref[rows, :], query[...]).astype(bf16)
                ref[t, p, :, width : width + LATENT] = mm_nt(dex_ref[rows, :], expand[...]).astype(
                    bf16
                )
                ref[t, p, :, width + LATENT : width + LATENT + ROPE] = d_rope[rows]
                if ref.shape[3] > width + LATENT + ROPE:
                    ref[t, p, :, width + LATENT + ROPE :] = jnp.zeros(
                        (n, ref.shape[3] - width - LATENT - ROPE), bf16
                    )


def attend_back(hd, lead, grad, out_w, prob, heads, ex, low, q, cos, sin, query, expand):
    cols = -(-(grad.shape[1] + LATENT + ROPE) // 128) * 128
    operands = (grad, out_w, prob, heads, ex, low, q, cos, sin, query, expand)
    out_shape = [
        (lead + (cols,), bf16),
        (lead + (cols,), bf16),
        (q.shape, bf16),
        (ex.shape, bf16),
    ]
    return whole_call(
        lambda *refs: attend_back_kernel(hd, *refs), operands, out_shape, "attend_back"
    )


def attend_weights_kernel(grad, heads, dq, normed, dex, low, dw_ref, de_ref):
    fs, _, dpart = dw_ref.shape
    first = heads.shape[1]
    for z in range(fs):
        at = slice(z * dpart, (z + 1) * dpart)
        dw_ref[z, :first] = mm_tn(heads[...], grad[:, at]).astype(bf16)
        dw_ref[z, first:] = mm_tn(dq[...], normed[:, at]).astype(bf16)
    de_ref[...] = mm_tn(low[:, :LATENT], dex[...]).astype(bf16)


def attend_weights(fs, grad, heads, dq, normed, dex, low):
    rows = heads.shape[1] + dq.shape[1]
    out_shape = [((fs, rows, grad.shape[1] // fs), bf16), ((LATENT, dex.shape[1]), bf16)]
    return whole_call(
        attend_weights_kernel,
        (grad, heads, dq, normed, dex, low),
        out_shape,
        "attend_weights",
        30_000_000,
    )


def weight_grads(left, right, fs, more=None, sh=0):
    slots, ffn = left.shape
    dpart = right.shape[1] // fs
    extra = 3 * sh if more is not None else 0
    once = pl.Buffered(buffer_count=1)

    def body(left_ref, right_ref, *refs):
        out_ref = refs[-1]
        out_ref[0, :ffn] = mm_tn(left_ref[...], right_ref[...]).astype(bf16)
        if more is not None:
            shp = more.shape[0] // 3
            for b in range(3):
                out_ref[0, ffn + b * sh : ffn + (b + 1) * sh] = refs[0][
                    b * shp : b * shp + sh
                ].astype(bf16)

    in_specs = [
        pl.BlockSpec((slots, ffn), lambda z: (0, 0), pipeline_mode=once),
        pl.BlockSpec((slots, dpart), lambda z: (0, z)),
    ]
    operands = [left, right]
    if more is not None:
        in_specs.append(pl.BlockSpec((more.shape[0], dpart), lambda z: (0, z)))
        operands.append(more)
    return pl.pallas_call(
        body,
        grid=(fs,),
        in_specs=in_specs,
        out_specs=pl.BlockSpec((1, ffn + extra, dpart), lambda z: (z, 0, 0)),
        out_shape=jax.ShapeDtypeStruct((fs, ffn + extra, dpart), bf16),
        compiler_params=pltpu.CompilerParams(vmem_limit_bytes=50 * 1024 * 1024),
        cost_estimate=pl.CostEstimate(flops=0, bytes_accessed=1_000_000, transcendentals=0),
        name="weight_grads",
    )(*operands)


def assemble(blocks, dest, count, rows):
    each, _, cols = blocks[0].shape
    parts = len(blocks)

    def body(dest_ref, *refs):
        step = pl.program_id(0)
        for q in range(parts):

            @pl.when(step // each == q)
            def _(q=q):
                refs[parts][...] = refs[q][...].astype(f32)

    def source(q):
        return pl.BlockSpec(
            (1, rows, cols), lambda g, dest: (jnp.clip(g - q * each, 0, each - 1), 0, 0)
        )

    return pl.pallas_call(
        body,
        grid_spec=pltpu.PrefetchScalarGridSpec(
            num_scalar_prefetch=1,
            grid=(parts * each,),
            in_specs=[source(q) for q in range(parts)],
            out_specs=pl.BlockSpec((1, rows, cols), lambda g, dest: (dest[g], 0, 0)),
        ),
        out_shape=jax.ShapeDtypeStruct((count, rows, cols), f32),
        compiler_params=pltpu.CompilerParams(vmem_limit_bytes=40 * 1024 * 1024),
        cost_estimate=pl.CostEstimate(flops=0, bytes_accessed=36_000_000, transcendentals=0),
        name="assemble",
    )(dest, *blocks)


def local(
    hidden_in,
    cotangent,
    routes,
    gate_weights,
    gain_attn,
    gain_latent,
    w_query,
    w_latent,
    w_expand,
    w_out,
    gain_moe,
    expert_gate,
    expert_up,
    expert_down,
    shared_gate,
    shared_up,
    shared_down,
):
    fs, cx, tp = lax.axis_size("fsdp"), lax.axis_size("ctx"), lax.axis_size("tp")
    i, j, k = lax.axis_index("fsdp"), lax.axis_index("ctx"), lax.axis_index("tp")
    rows_dev, width = hidden_in.shape
    n = rows_dev // tp
    length = rows_dev * cx
    dpart = width // fs
    q_width = NOPE + ROPE
    kv_width = NOPE + VHEAD
    heads_dev = w_out.shape[0] // VHEAD
    groups = min(cx, heads_dev)
    share = cx // groups
    hd = heads_dev // groups
    group = j // share
    lead = j % share == 0
    scaling = q_width ** (-0.5)
    assert EXPERTS == fs * cx

    members = [0]
    for bit in list(high_bits(cx)) + [1]:
        members = members + [m ^ bit for m in members]
    place_of = [members.index(m) for m in range(cx)]

    def spot(m):
        return jnp.asarray(place_of, jnp.int32)[m]

    def spread_ctx(cur):
        for bit in high_bits(cx):
            cur = jnp.concatenate([cur, exchange(cur, "ctx", bit)], axis=0)
        return cur

    def spread_core(cur):
        return jnp.concatenate([cur, exchange(cur, "ctx", 1)], axis=0)

    def spread_tp(cur):
        for bit in low_bits(tp):
            cur = jnp.concatenate([cur, exchange(cur, "tp", bit)], axis=1)
        return cur

    def gather_halves(own, ctx_first):
        cur = own[None, None]
        cur = spread_tp(spread_ctx(cur)) if ctx_first else spread_ctx(spread_tp(cur))
        return cur, exchange(cur, "ctx", 1)

    def gather_plane(own, ctx_first=True):
        return jnp.concatenate(gather_halves(own, ctx_first), axis=0)

    def gather_ctx(own):
        return spread_core(spread_ctx(own[None]))

    def over_ctx(stack, *pins):
        blocks = [stack]
        for bit in list(high_bits(cx)) + [1]:
            if bit == 1 and pins:
                blocks = [after(block, *pins) for block in blocks]
            blocks = blocks + [exchange(block, "ctx", bit) for block in blocks]
        return blocks

    def reduce_core(keep, send):
        return (keep.astype(f32) + exchange(send, "ctx", 1).astype(f32)).astype(bf16)

    def reduce_lead(cur, axis):
        bits = low_bits(tp) if axis == "tp" else high_bits(cx)
        for bit in sorted(bits, reverse=True):
            at = cur.shape[0] // 2
            other = exchange(cur[at:], axis, bit)
            cur = (cur[:at].astype(f32) + other.astype(f32)).astype(bf16)
        return cur[0]

    def reduce_plane(keep, send, *pins):
        cur = after(reduce_core(keep, send), *pins[:1])
        cur = after(reduce_lead(cur, "tp"), *pins[1:])
        return reduce_lead(cur, "ctx").astype(f32)

    def rel_tp(value):
        blocks = value.reshape((tp, n) + value.shape[1:])
        return jnp.concatenate(
            [lax.dynamic_index_in_dim(blocks, k ^ t, 0, keepdims=False) for t in range(tp)], axis=0
        )

    def own_rows(value):
        return lax.dynamic_slice_in_dim(value, k * n, n, 0)

    def hop(cur, bit):
        cur = cur.reshape((cur.shape[0] // 2, 2) + cur.shape[1:])
        mine = (i // bit) % 2
        send = lax.dynamic_index_in_dim(cur, 1 - mine, 1, keepdims=False).astype(bf16)
        keep = lax.dynamic_index_in_dim(cur, mine, 1, keepdims=False)
        return keep.astype(f32) + exchange(send, "fsdp", bit).astype(f32)

    def hops(cur, bits):
        for bit in bits:
            cur = hop(cur, bit)
        return cur

    def turn(value):
        return lax.all_to_all(value, "fsdp", 0, 0)

    hid_rel = rel_tp(hidden_in)
    x_rel = hid_rel[:n].astype(f32)
    hid_all = gather_ctx(hid_rel).reshape(length, width)
    row = jnp.arange(n, dtype=jnp.int32)
    pos_rel = jnp.concatenate(
        [(j ^ m) * rows_dev + (k ^ t) * n + row for m in members for t in range(tp)]
    )
    cos_rel, sin_rel = angle_tables(pos_rel, ROPE)
    hid_all = after(hid_all, cos_rel, sin_rel)

    lat_cols = w_latent.shape[1] // cx
    query_own = lax.dynamic_slice_in_dim(w_query, group * hd * q_width, hd * q_width, 1)
    latent_own = lax.dynamic_slice_in_dim(w_latent.T, j * lat_cols, lat_cols, 0)
    expand_own = lax.dynamic_slice_in_dim(w_expand, group * hd * kv_width, hd * kv_width, 1)
    out_own = lax.dynamic_slice_in_dim(w_out, group * hd * VHEAD, hd * VHEAD, 0)
    lat_part = gain_latent.shape[0]
    gate_high = lax.reduce_precision(gate_weights, 8, 7)
    gate_low = (gate_weights - gate_high).astype(bf16)
    small = jnp.concatenate(
        [routes.T.astype(bf16), gate_high.T.astype(bf16), gate_low.T], axis=0
    )
    small_rows = -(-small.size // dpart)
    small = rel_tp(small.T).T.reshape(-1)
    small = jnp.pad(small, (0, small_rows * dpart - small.shape[0])).reshape(small_rows, dpart)
    extra = jnp.concatenate(
        [
            gain_attn[None],
            gain_moe[None],
            jnp.pad(gain_latent, (0, dpart - lat_part))[None],
            small,
        ],
        axis=0,
    )
    extra = jnp.pad(extra, ((0, -extra.shape[0] % 16), (0, 0)))
    first_pack = jnp.concatenate([query_own.T, latent_own, extra], axis=0)
    first_pack = after(lax.all_gather(first_pack, "fsdp", axis=0), hid_all)
    q_cols = hd * q_width
    query_t = first_pack[:, :q_cols].transpose(1, 0, 2).reshape(q_cols, width)
    latent_t = first_pack[:, q_cols : q_cols + lat_cols].transpose(1, 0, 2)
    latent_t = gather_ctx(latent_t.reshape(lat_cols, width))
    latent_t = place(
        (cx * lat_cols, width), bf16, list(latent_t), [(j ^ m) * lat_cols for m in members], 0
    )
    extra = first_pack[:, q_cols + lat_cols :]
    gain_norm = extra[:, 0].reshape(-1).astype(f32)
    gain_mix = extra[:, 1].reshape(-1).astype(f32)
    gain_lat = extra[:, 2, :lat_part].reshape(-1).astype(f32)
    small = extra[:, 3 : 3 + small_rows].reshape(fs, -1)[:, : 3 * TOPK * rows_dev]
    small = gather_ctx(small.reshape(fs, 3 * TOPK, rows_dev))
    small = small.transpose(1, 0, 2, 3).reshape(fs * cx, 3 * TOPK, rows_dev).astype(f32)
    ex_rows = expand_own.size // dpart
    second_pack = lax.all_gather(
        after(
            jnp.concatenate([expand_own.reshape(ex_rows, dpart), out_own], axis=0), first_pack
        ),
        "fsdp",
        axis=0,
    )
    second_pack = after(second_pack, latent_t)
    expand_w = second_pack[:, :ex_rows].reshape(-1, hd * kv_width)
    output_w = second_pack[:, ex_rows:].transpose(1, 0, 2).reshape(hd * VHEAD, width)

    dy_own = own_rows(cotangent)
    dy_seqs = lax.all_gather(after(dy_own, second_pack), "fsdp", axis=0)

    sh = shared_gate.shape[1] // (cx * fs)
    shp = -(-sh // 128) * 128
    ffn = expert_down.shape[1]
    cut = j * fs * sh
    gate_w = turn(
        after(
            lax.dynamic_slice_in_dim(expert_gate.transpose(0, 2, 1), j * fs, fs, 0), second_pack
        )
    )
    shared_own = jnp.stack(
        [
            lax.dynamic_slice_in_dim(shared_gate, cut, fs * sh, 1).T.reshape(fs, sh, dpart),
            lax.dynamic_slice_in_dim(shared_up, cut, fs * sh, 1).T.reshape(fs, sh, dpart),
            lax.dynamic_slice_in_dim(shared_down, cut, fs * sh, 0).reshape(fs, sh, dpart),
        ],
        axis=1,
    )

    normed, attn_scale = norm_rows(hid_all.astype(f32), gain_norm)
    normed_all = normed.astype(bf16)
    expert = (j * fs + i).astype(f32)
    named = small[:, :TOPK] == expert
    chosen = jnp.any(named, axis=1).astype(f32)
    gates_all = small[:, TOPK : 2 * TOPK] + small[:, 2 * TOPK :]
    weight = jnp.sum(jnp.where(named, gates_all, 0.0), axis=1)
    ahead = (
        jnp.arange(rows_dev, dtype=jnp.int32)[:, None]
        < jnp.arange(rows_dev, dtype=jnp.int32)[None, :]
    ).astype(bf16)
    earlier = mm(chosen.astype(bf16), ahead).astype(jnp.int32)
    slot_of = jnp.where(chosen > 0.5, earlier, -1).reshape(fs * cx, 1, rows_dev)
    weight = weight.reshape(fs * cx, 1, rows_dev)
    slot_col = slot_of.reshape(fs * cx, rows_dev, 1)
    expand_w = after(expand_w, slot_of, slot_col, weight)

    keep, send, latent_raw, latent_low, queries, expanded, attn_prob, heads_out = attend(
        hd, (tp, cx // 2, n), normed_all, query_t, latent_t, expand_w, output_w, gain_lat, cos_rel, sin_rel, pos_rel
    )
    half = length // 2

    def leading(value):
        return value if share == 1 else jnp.where(lead, value, jnp.zeros((), value.dtype))

    attn_sum = after(reduce_plane(leading(keep), leading(send), dy_seqs), gate_w)
    middle = x_rel + attn_sum
    normed_moe, moe_scale = norm_rows(middle, gain_mix)
    moe_low = normed_moe.astype(bf16)

    per = fs // 2 if fs > 1 else 1
    row_seqs = lax.all_gather(moe_low, "fsdp", axis=0)

    def to_all(seqs, *pins):
        halves = []
        for g in range(fs // per):
            cur = seqs[g * per : (g + 1) * per][None, None]
            if g % 2 == 0:
                cur = spread_ctx(cur)
                cur = spread_tp(after(cur, *pins) if pins else cur)
            else:
                cur = spread_tp(cur)
                cur = spread_ctx(after(cur, *pins) if pins else cur)
            halves += [cur, exchange(cur, "ctx", 1)]
        return halves

    dy_halves = to_all(after(dy_seqs, middle), moe_low)
    up_w = turn(
        after(lax.dynamic_slice_in_dim(expert_up.transpose(0, 2, 1), j * fs, fs, 0), row_seqs)
    )
    row_halves = to_all(after(row_seqs, *dy_halves[::2]))
    shared_w = turn(after(shared_own, up_w))
    down_w = turn(after(lax.dynamic_slice_in_dim(expert_down, j * fs, fs, 0), shared_w))
    shared_w = shared_w.transpose(1, 2, 0, 3).reshape(3, sh, width)
    shared_w = jnp.pad(shared_w, ((0, 0), (0, shp - sh), (0, 0))).reshape(3 * shp, width)


    all_slots, all_dy, gate_act, up_act, shared_ds, d_shared = moe_rows(
        fs, ffn, row_halves, dy_halves, slot_of, shared_w, gate_w, up_w
    )
    me = jnp.zeros((1,), jnp.int32)

    name = (jnp.arange(128, dtype=jnp.int32) == j * fs + i).astype(f32)[None]
    big, flows = [], []
    dy_in = all_dy
    for g in range(fs // per):
        results = moe_back(
            g * per,
            per,
            tp,
            fs,
            g % 2 == 0,
            me,
            dy_in,
            gate_act,
            up_act,
            slot_of,
            slot_col,
            weight,
            shared_ds,
            shared_w,
            gate_w,
            up_w,
            down_w,
            name,
            big,
        )
        big = list(results[:3])
        dy_in = after(all_dy, results[4])
        flows.append(reduce_core(results[3], results[4]))
    all_dg, all_du, all_hw = big

    def split_cols(value):
        return value.reshape(value.shape[0], fs, dpart).transpose(1, 0, 2)

    d_gate_w = weight_grads(after(all_dg, *flows), all_slots, fs)
    gate_back = turn(d_gate_w)
    firsts = [reduce_lead(flow, "ctx" if g % 2 else "tp") for g, flow in enumerate(flows)]
    out_args = (slot_col, shared_ds, shared_w, down_w)
    outs = [
        moe_out(g * per, per, tp, fs, g % 2 == 1, me, after(all_hw, d_gate_w), *out_args)
        for g in range(fs // per)
    ]
    firsts = [after(flow, *outs[0], *outs[-1]) for flow in firsts]
    seconds = [reduce_lead(flow, "tp" if g % 2 else "ctx") for g, flow in enumerate(firsts)]
    home = after(jnp.concatenate(seconds, axis=0), gate_back)
    d_up_w = weight_grads(after(all_du, home), all_slots, fs)
    d_down_w = weight_grads(after(all_hw, home), all_dy, fs, d_shared, sh)
    out_flows = [
        reduce_lead(after(reduce_core(keep, send), home), "ctx" if g % 2 else "tp")
        for g, (keep, send) in enumerate(outs)
    ]
    home_own = jnp.sum(turn(home).astype(f32), axis=0)
    home_own = after(home_own, d_up_w, d_down_w, *out_flows)
    up_back = turn(after(d_up_w, home_own))
    grad_total, gate_cols = home_own[:, :width], home_own[:, width:]
    in_order = jnp.arange(EXPERTS, dtype=jnp.int32)

    def lay_out(blocks):
        return assemble([blocks.reshape(EXPERTS, -1, dpart)], in_order, EXPERTS, ffn)

    grad_mid_norm, d_gain_moe = norm_back(middle, moe_scale, gain_mix, grad_total)
    grad_mid = dy_own.astype(f32) + grad_mid_norm
    grad_low = grad_mid.astype(bf16)
    grad_cur = spread_ctx(grad_low[None, None])
    gate_blocks = lax.all_gather(after(gate_back, grad_cur), "ctx", axis=0)
    grad_all = spread_core(spread_tp(grad_cur)).reshape(length, width)

    down_back = turn(after(d_down_w, up_back))
    gate_shards = lay_out(gate_blocks)
    keep, send, grad_q, grad_expanded = attend_back(
        hd,
        (tp, cx // 2, n),
        grad_all,
        output_w,
        attn_prob,
        heads_out,
        expanded,
        latent_low,
        queries,
        cos_rel,
        sin_rel,
        query_t,
        expand_w,
    )
    up_blocks = lax.all_gather(after(up_back, grad_q), "ctx", axis=0)
    summed = reduce_plane(leading(keep), leading(send), up_back, gate_shards)
    out_flows = [
        reduce_lead(after(flow, summed), "tp" if g % 2 else "ctx")
        for g, flow in enumerate(out_flows)
    ]
    out_home = jnp.concatenate(out_flows, axis=0)
    d_attn, d_w_expand = attend_weights(
        fs, grad_all, heads_out, after(grad_q, send), normed_all, grad_expanded, latent_low
    )
    summed = after(summed, d_attn)
    grad_latent_own = summed[:, width : width + LATENT + ROPE]
    up_shards = lay_out(up_blocks)
    latent_scale = lax.rsqrt(
        jnp.mean(latent_raw[:n, :LATENT] ** 2, axis=-1, keepdims=True) + EPSILON
    )
    grad_lat_raw, d_gain_latent = norm_back(
        latent_raw[:n, :LATENT], latent_scale, gain_lat, grad_latent_own[:, :LATENT]
    )
    grad_kv_raw = jnp.concatenate(
        [grad_lat_raw, rotate_back(grad_latent_own[:, LATENT:], cos_rel[:n], sin_rel[:n])], axis=1
    ).astype(bf16)
    grad_normed = summed[:, :width] + mm(grad_kv_raw, latent_t)
    kv_all = gather_plane(grad_kv_raw).reshape(length, -1)
    d_w_latent = mm_tn(
        lax.dynamic_slice_in_dim(kv_all, j * lat_cols, lat_cols, 1), normed_all
    ).astype(bf16)
    ex_part = d_w_expand.size // (fs * dpart)
    pack = jnp.concatenate(
        [d_attn, d_w_expand.reshape(fs, ex_part, dpart), split_cols(d_w_latent)], axis=1
    )
    bits = list(low_bits(fs))
    pack_sum = hops(pack, bits[:1])
    out_sum = hops(after(out_home, pack_sum), bits[:1])
    pack_sum = after(pack_sum, up_shards)
    out_total = hops(out_sum, bits[1:])[0]
    down_blocks = lax.all_gather(after(down_back, d_w_latent), "ctx", axis=0)
    grad_x_norm, d_gain_attn = norm_back(x_rel, attn_scale[:n], gain_norm, grad_normed)
    input_own = (grad_mid + grad_x_norm).astype(bf16)
    input_grad = rel_tp(spread_tp(input_own[None, None]).reshape(rows_dev, width)).astype(f32)

    out_own_rows = (middle + out_total).astype(bf16)
    layer_out = rel_tp(spread_tp(out_own_rows[None, None]).reshape(rows_dev, width))

    gate_cols = spread_tp(gate_cols[:, :EXPERTS][None, None]).reshape(rows_dev, EXPERTS)
    gate_cols = rel_tp(gate_cols)
    experts = jnp.arange(EXPERTS, dtype=jnp.int32)
    gates_grad = jnp.sum(
        jnp.where(routes[:, :, None] == experts, gate_cols[:, None, :], 0.0), axis=-1
    )

    blocks = over_ctx(hops(pack_sum, bits[1:])[0].astype(bf16))
    at_q, at_e = hd * VHEAD, hd * VHEAD + q_cols
    by_group = [(j ^ m) // share for m in members]
    w_out_grad = place(
        w_out.shape, f32, [v[:at_q] for v in blocks], [g * hd * VHEAD for g in by_group], 0
    )
    w_query_grad = place(
        w_query.shape[::-1], f32, [v[at_q:at_e] for v in blocks], [g * q_cols for g in by_group], 0
    ).T
    w_expand_grad = place(
        w_expand.shape,
        f32,
        [
            v[at_e : at_e + ex_part].reshape(w_expand.shape[0], hd * kv_width) for v in blocks
        ],
        [g * hd * kv_width for g in by_group],
        1,
    )
    w_latent_grad = place(
        w_latent.shape[::-1],
        f32,
        [v[at_e + ex_part :] for v in blocks],
        [(j ^ m) * lat_cols for m in members],
        0,
    ).T

    gain_parts = jnp.concatenate(
        [
            d_gain_attn.reshape(fs, -1),
            d_gain_moe.reshape(fs, -1),
            d_gain_latent.reshape(fs, -1),
        ],
        axis=1,
    )
    gain_sum = jnp.sum(turn(gain_parts[:, None, :]), axis=0)
    for bit in low_bits(tp):
        gain_sum = gain_sum + exchange(gain_sum, "tp", bit)
    for bit in low_bits(cx):
        gain_sum = gain_sum + exchange(gain_sum, "ctx", bit)
    gain_sum = gain_sum[0]
    cut_a, cut_b = gain_attn.shape[0], gain_attn.shape[0] + gain_moe.shape[0]

    expert_gate_grad = gate_shards.transpose(0, 2, 1)
    expert_up_grad = up_shards.transpose(0, 2, 1)
    expert_down_grad = lay_out(down_blocks)
    shared_grads = down_blocks[:, :, ffn:].reshape(cx, fs, 3, sh, dpart).transpose(2, 0, 1, 3, 4)
    shared_grads = shared_grads.reshape(3, cx * fs * sh, dpart).astype(f32)
    shared_gate_grad = shared_grads[0].T
    shared_up_grad = shared_grads[1].T
    shared_down_grad = shared_grads[2]

    return (
        layer_out,
        input_grad,
        gates_grad,
        gain_sum[:cut_a],
        gain_sum[cut_b:],
        w_query_grad,
        w_latent_grad,
        w_expand_grad,
        w_out_grad,
        gain_sum[cut_a:cut_b],
        expert_gate_grad,
        expert_up_grad,
        expert_down_grad,
        shared_gate_grad,
        shared_up_grad,
        shared_down_grad,
    )


def solution(mesh):
    placed = (
        P(("fsdp", "ctx"), None),
        P(("fsdp", "ctx"), None),
        P(("fsdp", "ctx"), None),
        P(("fsdp", "ctx"), None),
        P("fsdp"),
        P("fsdp"),
        P("fsdp", "tp"),
        P("fsdp", None),
        P("fsdp", "tp"),
        P("tp", "fsdp"),
        P("fsdp"),
        P(None, "fsdp", "tp"),
        P(None, "fsdp", "tp"),
        P(None, "tp", "fsdp"),
        P("fsdp", "tp"),
        P("fsdp", "tp"),
        P("tp", "fsdp"),
    )
    return jax.shard_map(
        local,
        mesh=mesh,
        in_specs=placed,
        out_specs=(
            P(("fsdp", "ctx"), None),
            P(("fsdp", "ctx"), None),
            P(("fsdp", "ctx"), None),
            P("fsdp"),
            P("fsdp"),
            P("fsdp", "tp"),
            P("fsdp", None),
            P("fsdp", "tp"),
            P("tp", "fsdp"),
            P("fsdp"),
            P(None, "fsdp", "tp"),
            P(None, "fsdp", "tp"),
            P(None, "tp", "fsdp"),
            P("fsdp", "tp"),
            P("fsdp", "tp"),
            P("tp", "fsdp"),
        ),
        check_vma=False,
    )
```

profile of v0, /device:TPU:0, one launch (start us, length us, event | category | flops | bytes accessed | tf_op | source)
XLA Modules:
  0.0 1139.7 jit_solution(5124299021450779032)
XLA Ops:
  15.9 19.2 %collective-permute-done = bf16[1,256,2048]{2,1,0:T(8,128)(2,1)} collective-permute-done((bf16[1,256,2048]{2,1,0:T(8,128)(2,1)S(1)}, bf16[1,256,2048]{2,1,0:T(8,128)(2,1)}, u32[]{:S(2)}, u32[]{:S(2)}) %collective-permute-start) | collective-permute-done | bytes 1048608 | tf_op jit(solution)/shard_map/ppermute | solution.py:87
  52.3 12.4 %all-gather.15.cloned.1.call-done = bf16[2176,512]{1,0:T(8,128)(2,1)} async-done(((bf16[544,512]{1,0:T(8,128)(2,1)}), bf16[2176,512]{1,0:T(8,128)(2,1)}) %all-gather.15.cloned.1.call-update) | async-done | bytes 2228240 | tf_op jit(solution)/shard_map/all_gather | solution.py:831
  74.4 5.3 fusion.2.refs_0_.normed
  79.7 7.9 collective-permute-done.2
  97.9 10.8 all-gather.17.cloned.1.call-done
  114.4 23.3 %attend.1 = (bf16[2,2,128,2048]{3,2,1,0:T(8,128)(2,1)}, bf16[2,2,128,2048]{3,2,1,0:T(8,128)(2,1)}, f32[1024,576]{1,0:T(8,128)}, bf16[1024,576]{1,0:T(8,128)(2,1)...) custom-call(bf16[1024,2048]{1,0:T(8,128)(2,1)} %fusion.2.refs_0_.nor, ...), custom_call_target="tpu_custom_call" | custom-call | bytes 1000000 | tf_op jit(solution)/shard_map/attend/pallas_call | solution.py:483
  149.5 24.9 %all-gather.19.cloned.1.call-done = bf16[512,2048]{1,0:T(8,128)(2,1)} async-done(((bf16[128,2048]{1,0:T(8,128)(2,1)}), bf16[512,2048]{1,0:T(8,128)(2,1)}) %all-gather.19.cloned.1.call-update) | async-done | bytes 2097168 | tf_op jit(solution)/shard_map/all_gather | solution.py:859
  177.5 22.9 %collective-permute-done.7 = bf16[1,2,128,2048]{3,2,1,0:T(8,128)(2,1)S(1)} collective-permute-done((bf16[1,2,128,2048]{3,2,1,0:T(8,128)(2,1)S(1)}, bf16[1,2,128,2048]{3,2,1,0:T(8,128)(2,1)S(1)}, u32[]{:S(2)}, u32[]{:S(2)}) %collective-permute-start.7) | collective-permute-done | bytes 1048608 | tf_op jit(solution)/shard_map/ppermute | solution.py:87
  202.5 10.8 collective-permute-done.8
  225.9 22.1 %collective-permute-done.9 = bf16[1,1,2,128,2048]{4,3,2,1,0:T(8,128)(2,1)S(1)} collective-permute-done((bf16[1,1,2,128,2048]{4,3,2,1,0:T(8,128)(2,1)S(1)}, bf16[1,1,2,128,2048]{4,3,2,1,0:T(8,128)(2,1)S(1)}, u32[]{:S(2)}, u32[]{:S(2)}) %collective-permute-start.9) | collective-permute-done | bytes 1048608 | tf_op jit(solution)/shard_map/ppermute | solution.py:87
  257.6 8.5 all-gather.21.cloned.1.call-done
  276.1 20.5 %collective-permute-done.10 = bf16[2,1,2,128,2048]{4,3,2,1,0:T(8,128)(2,1)} collective-permute-done((bf16[2,1,2,128,2048]{4,3,2,1,0:T(8,128)(2,1)}, bf16[2,1,2,128,2048]{4,3,2,1,0:T(8,128)(2,1)}, u32[]{:S(2)}, u32[]{:S(2)}) %collective-permute-start.10) | collective-permute-done | bytes 2097184 | tf_op jit(solution)/shard_map/ppermute | solution.py:87
  306.4 20.4 %collective-permute-done.13 = bf16[1,1,2,128,2048]{4,3,2,1,0:T(8,128)(2,1)S(1)} collective-permute-done((bf16[1,1,2,128,2048]{4,3,2,1,0:T(8,128)(2,1)S(1)}, bf16[1,1,2,128,2048]{4,3,2,1,0:T(8,128)(2,1)S(1)}, u32[]{:S(2)}, u32[]{:S(2)}) %collective-permute-start.13) | collective-permute-done | bytes 1048608 | tf_op jit(solution)/shard_map/ppermute | solution.py:87
  353.8 19.9 %collective-permute-done.14 = bf16[2,1,2,128,2048]{4,3,2,1,0:T(8,128)(2,1)} collective-permute-done((bf16[2,1,2,128,2048]{4,3,2,1,0:T(8,128)(2,1)}, bf16[2,1,2,128,2048]{4,3,2,1,0:T(8,128)(2,1)}, u32[]{:S(2)}, u32[]{:S(2)}) %collective-permute-start.14) | collective-permute-done | bytes 2097184 | tf_op jit(solution)/shard_map/ppermute | solution.py:87
  392.3 47.3 %moe_rows.1 = (bf16[2048,2048]{1,0:T(8,128)(2,1)}, bf16[2048,2048]{1,0:T(8,128)(2,1)}, f32[2048,704]{1,0:T(8,128)}, f32[2048,704]{1,0:T(8,128)}, bf16[4096,384]{1,0:T(8,128)(2,1)}, /*index=5*/f32[384,2048]{1,0:T(8,128)}) custom-call(s32[16,1,256]{2,1,0:T(1,128)} %reshape.377.refs_0_.refs_4_, bf16[384,2048]{1,0:T(8,128)(2,1)} %bitcast.225, ...), custom_call_target="tpu_custom_call" | custom-call | bytes 1000000 | tf_op jit(solution)/shard_map/moe_rows/pallas_call | solution.py:215
  439.6 7.3 all-to-all-done.3.refs_11_.refs_5_
  448.5 34.2 %moe_back.2 = (bf16[2048,704]{1,0:T(8,128)(2,1)}, bf16[2048,704]{1,0:T(8,128)(2,1)}, bf16[2048,704]{1,0:T(8,128)(2,1)}, bf16[2,2,2,128,2176]{4,3,2,1,0:T(8,128)(2,1)}, bf16[2,2,2,128,2176]{4,3,2,1,0:T(8,128)(2,1)}) custom-call(s32[1]{0:T(128)} %constant.211.clone.1.refs_0_, bf16[2048,2048]{1,0:T(8,128)(2,1)} %get-tuple-element.113.refs_1_.right_ref, ...), custom_call_target="tpu_custom_call" | custom-call | bytes 1000000 | tf_op jit(solution)/shard_map/moe_back/pallas_call | solution.py:333
  482.7 34.3 %moe_back.3 = (bf16[2048,704]{1,0:T(8,128)(2,1)}, bf16[2048,704]{1,0:T(8,128)(2,1)}, bf16[2048,704]{1,0:T(8,128)(2,1)}, bf16[2,2,2,128,2176]{4,3,2,1,0:T(8,128)(2,1)}, bf16[2,2,2,128,2176]{4,3,2,1,0:T(8,128)(2,1)}) custom-call(s32[1]{0:T(128)} %constant.211.clone.1.refs_0_, ...), custom_call_target="tpu_custom_call", output_to_operand_aliasing={{0}: (13, {}), {1}: (14, {}), {2}: (15, {})} | custom-call | bytes 1000000 | tf_op jit(solution)/shard_map/moe_back/pallas_call | solution.py:333
  517.6 7.2 collective-permute-done.22
  536.1 10.0 weight_grads.3
  549.0 15.6 %moe_out.3 = (bf16[2,2,2,128,2048]{4,3,2,1,0:T(8,128)(2,1)}, bf16[2,2,2,128,2048]{4,3,2,1,0:T(8,128)(2,1)}) custom-call(s32[1]{0:T(128)} %constant.211.clone.1.refs_0_, bf16[2048,704]{1,0:T(8,128)(2,1)S(1)} %copy-done.10, s32[16,256,1]{2,1,0:T(8,128)S(1)} %copy-done.6, bf16[4096,384]{1,0:T(8,128)(2,1)S(1)} %copy-done.8, bf16[384,2048]{1,0:T(8,128)(2,1)S(1)} %bitcast.228, ...), custom_call_target="tpu_custom_call" | custom-call | bytes 1000000 | tf_op jit(solution)/shard_map/moe_out/pallas_call | solution.py:412
  564.6 5.1 all-to-all-start.4
  576.5 15.7 %moe_out.2 = (bf16[2,2,2,128,2048]{4,3,2,1,0:T(8,128)(2,1)}, bf16[2,2,2,128,2048]{4,3,2,1,0:T(8,128)(2,1)}) custom-call(s32[1]{0:T(128)} %constant.211.clone.1.refs_0_, bf16[2048,704]{1,0:T(8,128)(2,1)S(1)} %copy-done.11, s32[16,256,1]{2,1,0:T(8,128)S(1)} %copy-done.7, bf16[4096,384]{1,0:T(8,128)(2,1)S(1)} %copy-done.9, bf16[384,2048]{1,0:T(8,128)(2,1)S(1)} %bitcast.229, ...), custom_call_target="tpu_custom_call" | custom-call | bytes 1000000 | tf_op jit(solution)/shard_map/moe_out/pallas_call | solution.py:412
  600.7 21.4 %collective-permute-done.27 = bf16[1,2,128,2176]{3,2,1,0:T(8,128)(2,1)S(1)} collective-permute-done((bf16[1,2,128,2176]{3,2,1,0:T(8,128)(2,1)S(1)}, bf16[1,2,128,2176]{3,2,1,0:T(8,128)(2,1)S(1)}, u32[]{:S(2)}, u32[]{:S(2)}) %collective-permute-start.27) | collective-permute-done | bytes 1114144 | tf_op jit(solution)/shard_map/ppermute | solution.py:87
  629.1 6.1 add_convert_fusion.2
  651.4 10.5 weight_grads.4
  661.9 10.3 weight_grads.5
  672.2 19.0 %collective-permute-done.30 = bf16[1,2,2,128,2048]{4,3,2,1,0:T(8,128)(2,1)} collective-permute-done((bf16[1,2,2,128,2048]{4,3,2,1,0:T(8,128)(2,1)}, bf16[1,2,2,128,2048]{4,3,2,1,0:T(8,128)(2,1)}, u32[]{:S(2)}, u32[]{:S(2)}) %collective-permute-start.30) | collective-permute-done | bytes 2097184 | tf_op jit(solution)/shard_map/ppermute | solution.py:87
  706.4 11.3 collective-permute-done.31
  723.3 21.8 %collective-permute-done.32 = bf16[2,1,128,2048]{3,2,1,0:T(8,128)(2,1)S(1)} collective-permute-done((bf16[2,1,128,2048]{3,2,1,0:T(8,128)(2,1)S(1)}, bf16[2,1,128,2048]{3,2,1,0:T(8,128)(2,1)S(1)}, u32[]{:S(2)}, u32[]{:S(2)}) %collective-permute-start.32) | collective-permute-done | bytes 1048608 | tf_op jit(solution)/shard_map/ppermute | solution.py:87
  745.4 4.6 collective-permute-done.33
  752.4 21.6 %attend_back.1 = (bf16[2,2,128,2688]{3,2,1,0:T(8,128)(2,1)}, bf16[2,2,128,2688]{3,2,1,0:T(8,128)(2,1)}, bf16[1024,384]{1,0:T(8,128)(2,1)}, bf16[1024,512]{1,0:T(8,128)(2,1)}) custom-call(bf16[1024,2048]{1,0:T(8,128)(2,1)} %bitcast.230, bf16[256,2048]{1,0:T(8,128)(2,1)} %bitcast.241, bf16[2,1024,1024]{2,1,0:T(8,128)(2,1)} %get-tuple-element.139.refs_2_, ...), custom_call_target="tpu_custom_call" | custom-call | bytes 1000000 | tf_op jit(solution)/shard_map/attend_back/pallas_call | solution.py:483
  774.0 11.4 %all-to-all-done.6 = bf16[4,704,512]{2,1,0:T(8,128)(2,1)} async-done(((bf16[4,704,512]{2,1,0:T(8,128)(2,1)}), bf16[4,704,512]{2,1,0:T(8,128)(2,1)}, u32[]{:S(2)}, u32[]{:S(2)}) %all-to-all-start.6) | async-done | bytes 2883616 | tf_op jit(solution)/shard_map/all_to_all | solution.py:794
  785.6 5.3 collective-permute-done.34
  795.9 4.8 all-to-all-start.8
  800.8 26.6 %collective-permute-done.35 = bf16[1,2,128,2688]{3,2,1,0:T(8,128)(2,1)} collective-permute-done((bf16[1,2,128,2688]{3,2,1,0:T(8,128)(2,1)S(1)}, bf16[1,2,128,2688]{3,2,1,0:T(8,128)(2,1)}, u32[]{:S(2)}, u32[]{:S(2)}) %collective-permute-start.35) | collective-permute-done | bytes 1376288 | tf_op jit(solution)/shard_map/ppermute | solution.py:87
  833.9 10.6 assemble.3
  847.7 9.0 attend_weights.1
  856.7 21.3 %collective-permute-done.36 = bf16[1,128,2688]{2,1,0:T(8,128)(2,1)S(1)} collective-permute-done((bf16[1,128,2688]{2,1,0:T(8,128)(2,1)}, bf16[1,128,2688]{2,1,0:T(8,128)(2,1)S(1)}, u32[]{:S(2)}, u32[]{:S(2)}) %collective-permute-start.36) | collective-permute-done | bytes 688160 | tf_op jit(solution)/shard_map/ppermute | solution.py:87
  889.5 6.8 collective-permute-done.40
  921.1 5.4 all-to-all-start.7
  927.3 4.9 all-to-all-done.7
  944.5 40.5 %collective-permute-done.50 = f32[1,1152]{1,0:T(1,128)S(1)} collective-permute-done((f32[1,1152]{1,0:T(1,128)S(1)}, f32[1,1152]{1,0:T(1,128)S(1)}, u32[]{:S(2)}, u32[]{:S(2)}) %collective-permute-start.50) | collective-permute-done | bytes 4640 | tf_op jit(solution)/shard_map/ppermute | solution.py:87
  996.8 10.6 assemble.4
  1010.2 6.8 collective-permute-done.43
  1019.5 42.7 %collective-permute-done.51 = bf16[1,912,512]{2,1,0:T(8,128)(2,1)S(1)} collective-permute-done((bf16[1,912,512]{2,1,0:T(8,128)(2,1)S(1)}, bf16[1,912,512]{2,1,0:T(8,128)(2,1)S(1)}, u32[]{:S(2)}, u32[]{:S(2)}) %collective-permute-start.51) | collective-permute-done | bytes 933920 | tf_op jit(solution)/shard_map/ppermute | solution.py:87
  1073.3 7.9 collective-permute-done.52
  1116.1 16.3 %assemble.5 = f32[16,704,512]{2,1,0:T(8,128)} custom-call(s32[16]{0:T(128)S(1)} %iota.57.dest_ref, bf16[16,968,512]{2,1,0:T(8,128)(2,1)} %all-gather.27.cloned.1.call-done.refs_0_), custom_call_target="tpu_custom_call" | custom-call | bytes 36000000 | tf_op jit(solution)/shard_map/assemble/pallas_call | solution.py:665
  (493 shorter events, 360.3 us)
Async XLA Ops:
  7.3 57.4 %all-gather.15.cloned.1.call-start = ((), (), s32[]{:S(2)}) async-start(), calls=%async_computation.9 | async-start | bytes 2785280 | tf_op jit(solution)/shard_map/all_gather | solution.py:831
  8.8 26.3 %collective-permute-start = (bf16[1,256,2048]{2,1,0:T(8,128)(2,1)S(1)}, bf16[1,256,2048]{2,1,0:T(8,128)(2,1)}, u32[]{:S(2)}, u32[]{:S(2)}) collective-permute-start(bf16[1,256,2048]{2,1,0:T(8,128)(2,1)S(1)} %maximum_bitcast_fusion), channel_id=1, source_target_pairs={{0,4},{2,6},{4,0},{6,2},{1,5},{3,7},{5,1},{7,3},{8,12},{10,14},{12... | collective-permute-start | bytes 3145736 | tf_op jit(solution)/shard_map/ppermute | solution.py:87
  15.8 92.9 %all-gather.17.cloned.1.call-start = ((), (), s32[]{:S(2)}) async-start(), calls=%async_computation.10 | async-start | bytes 1966080 | tf_op jit(solution)/shard_map/all_gather | solution.py:847
  73.5 101.0 %all-gather.19.cloned.1.call-start = ((), (), s32[]{:S(2)}) async-start(), calls=%async_computation.11 | async-start | bytes 2621440 | tf_op jit(solution)/shard_map/all_gather | solution.py:859
  141.3 75.7 %all-to-all-start = ((bf16[4,704,512]{2,1,0:T(8,128)(2,1)}), bf16[4,704,512]{2,1,0:T(8,128)(2,1)S(1)}, u32[]{:S(2)}, u32[]{:S(2)}) async-start(bf16[4,704,512]{2,1,0:T(8,128)(2,1)} %dynamic-slice_bitcast_fusion.1), calls=%async_computation | async-start | bytes 5767168 | tf_op jit(solution)/shard_map/all_to_all | solution.py:794
  145.0 121.1 %all-gather.21.cloned.1.call-start = ((), (), s32[]{:S(2)}) async-start(), calls=%async_computation.12 | async-start | bytes 2621440 | tf_op jit(solution)/shard_map/all_gather | solution.py:910
  175.9 24.5 %collective-permute-start.7 = (bf16[1,2,128,2048]{3,2,1,0:T(8,128)(2,1)S(1)}, bf16[1,2,128,2048]{3,2,1,0:T(8,128)(2,1)S(1)}, u32[]{:S(2)}, u32[]{:S(2)}) collective-permute-start(bf16[1,2,128,2048]{3,2,1,0:T(8,128)(2,1)S(1)} %slice.260), channel_id=1, source_target_pairs={{0,1},{1,0},{2,3},{3,2},{4,5},{5,4},{6,7},{7,6},{8,9},{9,8},{10,11... | collective-permute-start | bytes 3145736 | tf_op jit(solution)/shard_map/ppermute | solution.py:87
  223.0 25.1 %collective-permute-start.9 = (bf16[1,1,2,128,2048]{4,3,2,1,0:T(8,128)(2,1)S(1)}, bf16[1,1,2,128,2048]{4,3,2,1,0:T(8,128)(2,1)S(1)}, u32[]{:S(2)}, u32[]{:S(2)}) collective-permute-start(bf16[1,1,2,128,2048]{4,3,2,1,0:T(8,128)(2,1)S(1)} %get-tuple-element.254), channel_id=1, source_target_pairs={{0,4},{2,6},{4,0},{6,2},{1,5},{3,7},{5,1},{7,3},{8,12},{10,14},{12... | collective-permute-start | bytes 3145736 | tf_op jit(solution)/shard_map/ppermute | solution.py:87
  224.5 26.5 %collective-permute-start.11 = (bf16[1,1,2,128,2048]{4,3,2,1,0:T(8,128)(2,1)S(1)}, bf16[1,1,2,128,2048]{4,3,2,1,0:T(8,128)(2,1)S(1)}, u32[]{:S(2)}, u32[]{:S(2)}) collective-permute-start(bf16[1,1,2,128,2048]{4,3,2,1,0:T(8,128)(2,1)S(1)} %get-tuple-element.253), channel_id=1, source_target_pairs={{0,1},{1,0},{2,3},{3,2},{4,5},{5,4},{6,7},{7,6},{8,9},{9,8},{10,11... | collective-permute-start | bytes 3145736 | tf_op jit(solution)/shard_map/ppermute | solution.py:87
  249.6 47.1 %collective-permute-start.10 = (bf16[2,1,2,128,2048]{4,3,2,1,0:T(8,128)(2,1)}, bf16[2,1,2,128,2048]{4,3,2,1,0:T(8,128)(2,1)}, u32[]{:S(2)}, u32[]{:S(2)}) collective-permute-start(bf16[2,1,2,128,2048]{4,3,2,1,0:T(8,128)(2,1)} %pad_maximum_fusion.7), channel_id=1, source_target_pairs={{0,1},{1,0},{2,3},{3,2},{4,5},{5,4},{6,7},{7,6},{8,9},{9,8},{10,11... | collective-permute-start | bytes 6291464 | tf_op jit(solution)/shard_map/ppermute | solution.py:87
  252.5 47.3 %collective-permute-start.12 = (bf16[1,2,2,128,2048]{4,3,2,1,0:T(8,128)(2,1)}, bf16[1,2,2,128,2048]{4,3,2,1,0:T(8,128)(2,1)}, u32[]{:S(2)}, u32[]{:S(2)}) collective-permute-start(bf16[1,2,2,128,2048]{4,3,2,1,0:T(8,128)(2,1)} %pad_maximum_fusion.8), channel_id=1, source_target_pairs={{0,4},{2,6},{4,0},{6,2},{1,5},{3,7},{5,1},{7,3},{8,12},{10,14},{12... | collective-permute-start | bytes 6291464 | tf_op jit(solution)/shard_map/ppermute | solution.py:87
  266.1 76.1 %all-to-all-start.1 = ((bf16[4,704,512]{2,1,0:T(8,128)(2,1)}), bf16[4,704,512]{2,1,0:T(8,128)(2,1)S(1)}, u32[]{:S(2)}, u32[]{:S(2)}) async-start(bf16[4,704,512]{2,1,0:T(8,128)(2,1)} %dynamic-slice_bitcast_fusion), calls=%async_computation.1 | async-start | bytes 5767168 | tf_op jit(solution)/shard_map/all_to_all | solution.py:794
  303.4 23.4 %collective-permute-start.13 = (bf16[1,1,2,128,2048]{4,3,2,1,0:T(8,128)(2,1)S(1)}, bf16[1,1,2,128,2048]{4,3,2,1,0:T(8,128)(2,1)S(1)}, u32[]{:S(2)}, u32[]{:S(2)}) collective-permute-start(bf16[1,1,2,128,2048]{4,3,2,1,0:T(8,128)(2,1)S(1)} %get-tuple-element.252), channel_id=1, source_target_pairs={{0,4},{2,6},{4,0},{6,2},{1,5},{3,7},{5,1},{7,3},{8,12},{10,14},{12... | collective-permute-start | bytes 3145736 | tf_op jit(solution)/shard_map/ppermute | solution.py:87
  304.9 25.0 %collective-permute-start.16 = (bf16[1,1,2,128,2048]{4,3,2,1,0:T(8,128)(2,1)S(1)}, bf16[1,1,2,128,2048]{4,3,2,1,0:T(8,128)(2,1)S(1)}, u32[]{:S(2)}, u32[]{:S(2)}) collective-permute-start(bf16[1,1,2,128,2048]{4,3,2,1,0:T(8,128)(2,1)S(1)} %get-tuple-element.251), channel_id=1, source_target_pairs={{0,1},{1,0},{2,3},{3,2},{4,5},{5,4},{6,7},{7,6},{8,9},{9,8},{10,11... | collective-permute-start | bytes 3145736 | tf_op jit(solution)/shard_map/ppermute | solution.py:87
  328.5 45.2 %collective-permute-start.14 = (bf16[2,1,2,128,2048]{4,3,2,1,0:T(8,128)(2,1)}, bf16[2,1,2,128,2048]{4,3,2,1,0:T(8,128)(2,1)}, u32[]{:S(2)}, u32[]{:S(2)}) collective-permute-start(bf16[2,1,2,128,2048]{4,3,2,1,0:T(8,128)(2,1)} %pad_maximum_fusion.9), channel_id=1, source_target_pairs={{0,1},{1,0},{2,3},{3,2},{4,5},{5,4},{6,7},{7,6},{8,9},{9,8},{10,11... | collective-permute-start | bytes 6291464 | tf_op jit(solution)/shard_map/ppermute | solution.py:87
  332.4 48.6 %collective-permute-start.17 = (bf16[1,2,2,128,2048]{4,3,2,1,0:T(8,128)(2,1)}, bf16[1,2,2,128,2048]{4,3,2,1,0:T(8,128)(2,1)}, u32[]{:S(2)}, u32[]{:S(2)}) collective-permute-start(bf16[1,2,2,128,2048]{4,3,2,1,0:T(8,128)(2,1)} %pad_maximum_fusion.10), channel_id=1, source_target_pairs={{0,4},{2,6},{4,0},{6,2},{1,5},{3,7},{5,1},{7,3},{8,12},{10,14},{12... | collective-permute-start | bytes 6291464 | tf_op jit(solution)/shard_map/ppermute | solution.py:87
  345.3 31.8 %all-to-all-start.2 = ((bf16[4,3,88,512]{3,2,1,0:T(8,128)(2,1)}), bf16[4,3,88,512]{3,2,1,0:T(8,128)(2,1)}, u32[]{:S(2)}, u32[]{:S(2)}) async-start(bf16[4,3,88,512]{3,2,1,0:T(8,128)(2,1)} %copy.147), calls=%async_computation.2 | async-start | bytes 2162688 | tf_op jit(solution)/shard_map/all_to_all | solution.py:794
  353.3 37.0 %collective-permute-start.19 = (bf16[2,2,2,128,2048]{4,3,2,1,0:T(8,128)(2,1)}, bf16[2,2,2,128,2048]{4,3,2,1,0:T(8,128)(2,1)}, u32[]{:S(2)}, u32[]{:S(2)}) collective-permute-start(bf16[2,2,2,128,2048]{4,3,2,1,0:T(8,128)(2,1)} %constant_dynamic-update-slice_fusion.6.refs_6_), channel_id=1, source_target_pairs={{0,2},{2,0},{4,6},{6,4},{1,3},{3,1},{5,7},{7,5},{8,10},{10,8},{12,... | collective-permute-start | bytes 12582920 | tf_op jit(solution)/shard_map/ppermute | solution.py:87
  353.3 37.0 %collective-permute-start.20 = (bf16[2,2,2,128,2048]{4,3,2,1,0:T(8,128)(2,1)}, bf16[2,2,2,128,2048]{4,3,2,1,0:T(8,128)(2,1)}, u32[]{:S(2)}, u32[]{:S(2)}) collective-permute-start(bf16[2,2,2,128,2048]{4,3,2,1,0:T(8,128)(2,1)} %constant_dynamic-update-slice_fusion.8.refs_8_), channel_id=1, source_target_pairs={{0,2},{2,0},{4,6},{6,4},{1,3},{3,1},{5,7},{7,5},{8,10},{10,8},{12,... | collective-permute-start | bytes 12582920 | tf_op jit(solution)/shard_map/ppermute | solution.py:87
  377.1 69.8 %all-to-all-start.3 = ((bf16[4,704,512]{2,1,0:T(8,128)(2,1)}), bf16[4,704,512]{2,1,0:T(8,128)(2,1)S(1)}, u32[]{:S(2)}, u32[]{:S(2)}) async-start(bf16[4,704,512]{2,1,0:T(8,128)(2,1)} %constant_dynamic-slice_fusion), calls=%async_computation.3 | async-start | bytes 5767168 | tf_op jit(solution)/shard_map/all_to_all | solution.py:794
  530.1 62.5 %collective-permute-start.26 = (bf16[1,2,2,128,2176]{4,3,2,1,0:T(8,128)(2,1)}, bf16[1,2,2,128,2176]{4,3,2,1,0:T(8,128)(2,1)}, u32[]{:S(2)}, u32[]{:S(2)}) collective-permute-start(bf16[1,2,2,128,2176]{4,3,2,1,0:T(8,128)(2,1)} %slice.333), channel_id=1, source_target_pairs={{0,4},{2,6},{4,0},{6,2},{1,5},{3,7},{5,1},{7,3},{8,12},{10,14},{12... | collective-permute-start | bytes 6684680 | tf_op jit(solution)/shard_map/ppermute | solution.py:87
  534.6 62.1 %collective-permute-start.24 = (bf16[1,2,2,128,2176]{4,3,2,1,0:T(8,128)(2,1)}, bf16[1,2,2,128,2176]{4,3,2,1,0:T(8,128)(2,1)}, u32[]{:S(2)}, u32[]{:S(2)}) collective-permute-start(bf16[1,2,2,128,2176]{4,3,2,1,0:T(8,128)(2,1)} %slice.331), channel_id=1, source_target_pairs={{0,1},{1,0},{2,3},{3,2},{4,5},{5,4},{6,7},{7,6},{8,9},{9,8},{10,11... | collective-permute-start | bytes 6684680 | tf_op jit(solution)/shard_map/ppermute | solution.py:87
  564.6 63.1 %collective-permute-start.29 = (bf16[2,2,2,128,2048]{4,3,2,1,0:T(8,128)(2,1)}, bf16[2,2,2,128,2048]{4,3,2,1,0:T(8,128)(2,1)}, u32[]{:S(2)}, u32[]{:S(2)}) collective-permute-start(bf16[2,2,2,128,2048]{4,3,2,1,0:T(8,128)(2,1)} %get-tuple-element.128), channel_id=1, source_target_pairs={{0,2},{2,0},{4,6},{6,4},{1,3},{3,1},{5,7},{7,5},{8,10},{10,8},{12,... | collective-permute-start | bytes 12582920 | tf_op jit(solution)/shard_map/ppermute | solution.py:87
  564.6 71.1 %all-to-all-start.4 = ((bf16[4,704,512]{2,1,0:T(8,128)(2,1)}), bf16[4,704,512]{2,1,0:T(8,128)(2,1)}, u32[]{:S(2)}, u32[]{:S(2)}) async-start(bf16[4,704,512]{2,1,0:T(8,128)(2,1)} %copy-done.13), calls=%async_computation.4 | async-start | bytes 5767168 | tf_op jit(solution)/shard_map/all_to_all | solution.py:794
  592.1 52.7 %collective-permute-start.23 = (bf16[2,2,2,128,2048]{4,3,2,1,0:T(8,128)(2,1)}, bf16[2,2,2,128,2048]{4,3,2,1,0:T(8,128)(2,1)}, u32[]{:S(2)}, u32[]{:S(2)}) collective-permute-start(bf16[2,2,2,128,2048]{4,3,2,1,0:T(8,128)(2,1)} %get-tuple-element.126), channel_id=1, source_target_pairs={{0,2},{2,0},{4,6},{6,4},{1,3},{3,1},{5,7},{7,5},{8,10},{10,8},{12,... | collective-permute-start | bytes 12582920 | tf_op jit(solution)/shard_map/ppermute | solution.py:87
  595.5 26.5 %collective-permute-start.27 = (bf16[1,2,128,2176]{3,2,1,0:T(8,128)(2,1)S(1)}, bf16[1,2,128,2176]{3,2,1,0:T(8,128)(2,1)S(1)}, u32[]{:S(2)}, u32[]{:S(2)}) collective-permute-start(bf16[1,2,128,2176]{3,2,1,0:T(8,128)(2,1)S(1)} %slice.275), channel_id=1, source_target_pairs={{0,1},{1,0},{2,3},{3,2},{4,5},{5,4},{6,7},{7,6},{8,9},{9,8},{10,11... | collective-permute-start | bytes 3342344 | tf_op jit(solution)/shard_map/ppermute | solution.py:87
  599.5 26.3 %collective-permute-start.25 = (bf16[1,2,128,2176]{3,2,1,0:T(8,128)(2,1)S(1)}, bf16[1,2,128,2176]{3,2,1,0:T(8,128)(2,1)S(1)}, u32[]{:S(2)}, u32[]{:S(2)}) collective-permute-start(bf16[1,2,128,2176]{3,2,1,0:T(8,128)(2,1)S(1)} %slice.271), channel_id=1, source_target_pairs={{0,4},{2,6},{4,0},{6,2},{1,5},{3,7},{5,1},{7,3},{8,12},{10,14},{12... | collective-permute-start | bytes 3342344 | tf_op jit(solution)/shard_map/ppermute | solution.py:87
  635.7 65.7 %all-to-all-start.5 = ((bf16[4,128,2176]{2,1,0:T(8,128)(2,1)}), bf16[4,128,2176]{2,1,0:T(8,128)(2,1)}, u32[]{:S(2)}, u32[]{:S(2)}) async-start(bf16[4,128,2176]{2,1,0:T(8,128)(2,1)} %pad_maximum_fusion.5), calls=%async_computation.5 | async-start | bytes 4456448 | tf_op jit(solution)/shard_map/all_to_all | solution.py:794
  640.2 189.2 %all-gather.23.cloned.1.call-start = ((), (), s32[]{:S(2)}) async-start(), calls=%async_computation.13 | async-start | bytes 14417920 | tf_op jit(solution)/shard_map/all_gather | solution.py:1004
  643.6 47.6 %collective-permute-start.30 = (bf16[1,2,2,128,2048]{4,3,2,1,0:T(8,128)(2,1)}, bf16[1,2,2,128,2048]{4,3,2,1,0:T(8,128)(2,1)}, u32[]{:S(2)}, u32[]{:S(2)}) collective-permute-start(bf16[1,2,2,128,2048]{4,3,2,1,0:T(8,128)(2,1)} %slice.279), channel_id=1, source_target_pairs={{0,4},{2,6},{4,0},{6,2},{1,5},{3,7},{5,1},{7,3},{8,12},{10,14},{12... | collective-permute-start | bytes 6291464 | tf_op jit(solution)/shard_map/ppermute | solution.py:87
  650.5 47.2 %collective-permute-start.28 = (bf16[1,2,2,128,2048]{4,3,2,1,0:T(8,128)(2,1)}, bf16[1,2,2,128,2048]{4,3,2,1,0:T(8,128)(2,1)}, u32[]{:S(2)}, u32[]{:S(2)}) collective-permute-start(bf16[1,2,2,128,2048]{4,3,2,1,0:T(8,128)(2,1)} %slice.277), channel_id=1, source_target_pairs={{0,1},{1,0},{2,3},{3,2},{4,5},{5,4},{6,7},{7,6},{8,9},{9,8},{10,11... | collective-permute-start | bytes 6291464 | tf_op jit(solution)/shard_map/ppermute | solution.py:87
  717.8 67.7 %all-to-all-start.6 = ((bf16[4,704,512]{2,1,0:T(8,128)(2,1)}), bf16[4,704,512]{2,1,0:T(8,128)(2,1)}, u32[]{:S(2)}, u32[]{:S(2)}) async-start(bf16[4,704,512]{2,1,0:T(8,128)(2,1)} %weight_grads.4), calls=%async_computation.6 | async-start | bytes 5767168 | tf_op jit(solution)/shard_map/all_to_all | solution.py:794
  722.4 270.1 %all-gather.25.cloned.1.call-start = ((), (), s32[]{:S(2)}) async-start(), calls=%async_computation.14 | async-start | bytes 14417920 | tf_op jit(solution)/shard_map/all_gather | solution.py:1024
  722.5 22.6 %collective-permute-start.32 = (bf16[2,1,128,2048]{3,2,1,0:T(8,128)(2,1)S(1)}, bf16[2,1,128,2048]{3,2,1,0:T(8,128)(2,1)S(1)}, u32[]{:S(2)}, u32[]{:S(2)}) collective-permute-start(bf16[2,1,128,2048]{3,2,1,0:T(8,128)(2,1)S(1)} %pad_maximum_fusion.16), channel_id=1, source_target_pairs={{0,1},{1,0},{2,3},{3,2},{4,5},{5,4},{6,7},{7,6},{8,9},{9,8},{10,11... | collective-permute-start | bytes 3145736 | tf_op jit(solution)/shard_map/ppermute | solution.py:87
  795.0 32.4 %collective-permute-start.35 = (bf16[1,2,128,2688]{3,2,1,0:T(8,128)(2,1)S(1)}, bf16[1,2,128,2688]{3,2,1,0:T(8,128)(2,1)}, u32[]{:S(2)}, u32[]{:S(2)}) collective-permute-start(bf16[1,2,128,2688]{3,2,1,0:T(8,128)(2,1)S(1)} %slice.282), channel_id=1, source_target_pairs={{0,1},{1,0},{2,3},{3,2},{4,5},{5,4},{6,7},{7,6},{8,9},{9,8},{10,11... | collective-permute-start | bytes 4128776 | tf_op jit(solution)/shard_map/ppermute | solution.py:87
  795.9 109.4 %all-to-all-start.8 = ((bf16[4,968,512]{2,1,0:T(8,128)(2,1)}), bf16[4,968,512]{2,1,0:T(8,128)(2,1)}, u32[]{:S(2)}, u32[]{:S(2)}) async-start(bf16[4,968,512]{2,1,0:T(8,128)(2,1)} %weight_grads.5), calls=%async_computation.8 | async-start | bytes 7929856 | tf_op jit(solution)/shard_map/all_to_all | solution.py:794
  800.7 302.5 %all-gather.27.cloned.1.call-start = ((), (), s32[]{:S(2)}) async-start(), calls=%async_computation.15 | async-start | bytes 19824640 | tf_op jit(solution)/shard_map/all_gather | solution.py:1060
  845.4 32.7 %collective-permute-start.36 = (bf16[1,128,2688]{2,1,0:T(8,128)(2,1)}, bf16[1,128,2688]{2,1,0:T(8,128)(2,1)S(1)}, u32[]{:S(2)}, u32[]{:S(2)}) collective-permute-start(bf16[1,128,2688]{2,1,0:T(8,128)(2,1)} %slice.284), channel_id=1, source_target_pairs={{0,4},{2,6},{4,0},{6,2},{1,5},{3,7},{5,1},{7,3},{8,12},{10,14},{12... | collective-permute-start | bytes 2064392 | tf_op jit(solution)/shard_map/ppermute | solution.py:87
  935.5 49.4 %collective-permute-start.38 = (bf16[1,2,128,2048]{3,2,1,0:T(8,128)(2,1)S(1)}, bf16[1,2,128,2048]{3,2,1,0:T(8,128)(2,1)S(1)}, u32[]{:S(2)}, u32[]{:S(2)}) collective-permute-start(bf16[1,2,128,2048]{3,2,1,0:T(8,128)(2,1)S(1)} %slice.288), channel_id=1, source_target_pairs={{0,1},{1,0},{2,3},{3,2},{4,5},{5,4},{6,7},{7,6},{8,9},{9,8},{10,11... | collective-permute-start | bytes 3145736 | tf_op jit(solution)/shard_map/ppermute | solution.py:87
  937.2 48.1 %collective-permute-start.37 = (bf16[1,2,128,2048]{3,2,1,0:T(8,128)(2,1)S(1)}, bf16[1,2,128,2048]{3,2,1,0:T(8,128)(2,1)S(1)}, u32[]{:S(2)}, u32[]{:S(2)}) collective-permute-start(bf16[1,2,128,2048]{3,2,1,0:T(8,128)(2,1)S(1)} %slice.286), channel_id=1, source_target_pairs={{0,4},{2,6},{4,0},{6,2},{1,5},{3,7},{5,1},{7,3},{8,12},{10,14},{12... | collective-permute-start | bytes 3145736 | tf_op jit(solution)/shard_map/ppermute | solution.py:87
  941.0 44.9 %collective-permute-start.42 = (bf16[2,912,512]{2,1,0:T(8,128)(2,1)S(1)}, bf16[2,912,512]{2,1,0:T(8,128)(2,1)S(1)}, u32[]{:S(2)}, u32[]{:S(2)}) collective-permute-start(bf16[2,912,512]{2,1,0:T(8,128)(2,1)S(1)} %dynamic-slice_bitcast_fusion.2), channel_id=1, source_target_pairs={{0,8},{8,0},{16,24},{24,16},{1,9},{9,1},{17,25},{25,17},{2,10},{10... | collective-permute-start | bytes 5603336 | tf_op jit(solution)/shard_map/ppermute | solution.py:87
  941.8 43.1 %collective-permute-start.50 = (f32[1,1152]{1,0:T(1,128)S(1)}, f32[1,1152]{1,0:T(1,128)S(1)}, u32[]{:S(2)}, u32[]{:S(2)}) collective-permute-start(f32[1,1152]{1,0:T(1,128)S(1)} %add.432), channel_id=1, source_target_pairs={{0,4},{2,6},{4,0},{6,2},{1,5},{3,7},{5,1},{7,3},{8,12},{10,14},{12... | collective-permute-start | bytes 13832 | tf_op jit(solution)/shard_map/ppermute | solution.py:87
  943.9 47.2 %collective-permute-start.46 = (bf16[1,1,128,2048]{3,2,1,0:T(8,128)(2,1)S(1)}, bf16[1,1,128,2048]{3,2,1,0:T(8,128)(2,1)S(1)}, u32[]{:S(2)}, u32[]{:S(2)}) collective-permute-start(bf16[1,1,128,2048]{3,2,1,0:T(8,128)(2,1)S(1)} %fusion.29), channel_id=1, source_target_pairs={{0,1},{1,0},{2,3},{3,2},{4,5},{5,4},{6,7},{7,6},{8,9},{9,8},{10,11... | collective-permute-start | bytes 1572872 | tf_op jit(solution)/shard_map/ppermute | solution.py:87
  989.4 27.5 %collective-permute-start.43 = (bf16[2,128,2048]{2,1,0:T(8,128)(2,1)}, bf16[2,128,2048]{2,1,0:T(8,128)(2,1)}, u32[]{:S(2)}, u32[]{:S(2)}) collective-permute-start(bf16[2,128,2048]{2,1,0:T(8,128)(2,1)} %dynamic-slice_bitcast_fusion.3), channel_id=1, source_target_pairs={{0,8},{8,0},{16,24},{24,16},{1,9},{9,1},{17,25},{25,17},{2,10},{10... | collective-permute-start | bytes 3145736 | tf_op jit(solution)/shard_map/ppermute | solution.py:87
  1007.5 54.7 %collective-permute-start.51 = (bf16[1,912,512]{2,1,0:T(8,128)(2,1)S(1)}, bf16[1,912,512]{2,1,0:T(8,128)(2,1)S(1)}, u32[]{:S(2)}, u32[]{:S(2)}) collective-permute-start(bf16[1,912,512]{2,1,0:T(8,128)(2,1)S(1)} %dynamic-slice_convert_fusion), channel_id=1, source_target_pairs={{0,16},{8,24},{16,0},{24,8},{1,17},{9,25},{17,1},{25,9},{2,18},{10... | collective-permute-start | bytes 2801672 | tf_op jit(solution)/shard_map/ppermute | solution.py:87
  1019.5 52.0 %collective-permute-start.44 = (bf16[1,128,2048]{2,1,0:T(8,128)(2,1)}, bf16[1,128,2048]{2,1,0:T(8,128)(2,1)}, u32[]{:S(2)}, u32[]{:S(2)}) collective-permute-start(bf16[1,128,2048]{2,1,0:T(8,128)(2,1)} %dynamic-slice_convert_fusion.1), channel_id=1, source_target_pairs={{0,16},{8,24},{16,0},{24,8},{1,17},{9,25},{17,1},{25,9},{2,18},{10... | collective-permute-start | bytes 1572872 | tf_op jit(solution)/shard_map/ppermute | solution.py:87
  1062.5 18.7 %collective-permute-start.52 = (bf16[912,512]{1,0:T(8,128)(2,1)S(1)}, bf16[912,512]{1,0:T(8,128)(2,1)}, u32[]{:S(2)}, u32[]{:S(2)}) collective-permute-start(bf16[912,512]{1,0:T(8,128)(2,1)S(1)} %bitcast.253), channel_id=1, source_target_pairs={{0,4},{2,6},{4,0},{6,2},{1,5},{3,7},{5,1},{7,3},{8,12},{10,14},{12... | collective-permute-start | bytes 2801672 | tf_op jit(solution)/shard_map/ppermute | solution.py:87
  1072.7 23.4 %collective-permute-start.45 = (bf16[1,1,128,2048]{3,2,1,0:T(8,128)(2,1)S(1)}, bf16[1,1,128,2048]{3,2,1,0:T(8,128)(2,1)}, u32[]{:S(2)}, u32[]{:S(2)}) collective-permute-start(bf16[1,1,128,2048]{3,2,1,0:T(8,128)(2,1)S(1)} %fusion.28), channel_id=1, source_target_pairs={{0,1},{1,0},{2,3},{3,2},{4,5},{5,4},{6,7},{7,6},{8,9},{9,8},{10,11... | collective-permute-start | bytes 1572872 | tf_op jit(solution)/shard_map/ppermute | solution.py:87
  (101 other events, 1117.9 us)
Sparse Core Ops, SparseCore 0:
  16.0 48.6 all-gather.14
  73.6 35.0 all-gather.16
  110.8 63.5 all-gather.18
  221.4 44.6 all-gather.20
  717.9 75.9 all-gather.22
  795.3 91.4 all-gather.24
  905.4 124.0 all-gather.26
where the time goes:
time: 1150 us; the launch traced here: 1140 us
  waiting for transfers between devices  487 us (42%)
  Pallas kernels  269 us (23%)
  local copies, waits for them, and re-layouts  136 us (12%)
  other arithmetic  135 us (12%)
  starting transfers between devices  88.7 us (8%)
  between operations  16.3 us (1%)
    ppermute x55, waiting for transfers between devices, exchange(): return lax.ppermute(value, axis, [(a, a ^ bit) for a in range(size)])  403 us
    pallas_call x2, Pallas kernels, moe_back(): pl.pallas_call(lambda *refs: back_kernel(pieces, fs, len(big), tp_first,...  68.5 us
    pallas_call x3, Pallas kernels, whole_call(): pl.pallas_call(body, in_specs=[pl.BlockSpec(memory_space=pltpu.VMEM)] * l...  54 us
    ppermute x55, starting transfers between devices, exchange(): return lax.ppermute(value, axis, [(a, a ^ bit) for a in range(size)])  48.3 us
    pallas_call x1, Pallas kernels, moe_rows(): pl.pallas_call(lambda *refs: rows_kernel(pieces, fs, steps, groups, *refs...  47.3 us
    unnamed x166, local copies, waits for them, and re-layouts  46.4 us
    all_to_all x9, starting transfers between devices, turn(): return lax.all_to_all(value, 'fsdp', 0, 0)  39.9 us
    pallas_call x3, Pallas kernels, assemble(): pl.pallas_call(body, grid_spec=pltpu.PrefetchScalarGridSpec(num_scalar_pr...  37.5 us
  transfers between devices with their start and end apart: 71, of which 37 were waited for; matrix products, arithmetic and copies ran while one was open for 20% of the time, Pallas kernels for 16%

commit v1 on v0

--- a/solution.py
+++ b/solution.py
@@ -1056,6 +1056,7 @@
     pack_sum = hops(pack, bits[:1])
     out_sum = hops(after(out_home, pack_sum), bits[:1])
     pack_sum = after(pack_sum, up_shards)
+    pack_total = hops(pack_sum, bits[1:])[0]
     out_total = hops(out_sum, bits[1:])[0]
     down_blocks = lax.all_gather(after(down_back, d_w_latent), "ctx", axis=0)
     grad_x_norm, d_gain_attn = norm_back(x_rel, attn_scale[:n], gain_norm, grad_normed)
@@ -1072,7 +1073,7 @@
         jnp.where(routes[:, :, None] == experts, gate_cols[:, None, :], 0.0), axis=-1
     )
 
-    blocks = over_ctx(hops(pack_sum, bits[1:])[0].astype(bf16))
+    blocks = over_ctx(pack_total.astype(bf16))
     at_q, at_e = hd * VHEAD, hd * VHEAD + q_cols
     by_group = [(j ^ m) // share for m in members]
     w_out_grad = place(
@@ -1106,7 +1107,7 @@
         ],
         axis=1,
     )
-    gain_sum = jnp.sum(turn(gain_parts[:, None, :]), axis=0)
+    gain_sum = jnp.sum(turn(after(gain_parts[:, None, :], pack_total)), axis=0)
     for bit in low_bits(tp):
         gain_sum = gain_sum + exchange(gain_sum, "tp", bit)
     for bit in low_bits(cx):

time: 1150 us -> 1140 us (level)
  waiting for transfers between devices: 487 us -> 474 us
    unnamed x166 -> x172, local copies, waits for them, and re-layouts: 46.4 us -> 46.3 us
  transfers between devices with their start and end apart: 71 -> 71, of which waited for: 37 -> 38; matrix products, arithmetic and copies ran while one was open for 20% -> 19% of each run, Pallas kernels for 16% -> 16%
where the time goes in v1:
time: 1140 us; the launch traced here: 1130 us
  waiting for transfers between devices  474 us (42%)
  Pallas kernels  269 us (24%)
  local copies, waits for them, and re-layouts  137 us (12%)
  other arithmetic  133 us (12%)
  starting transfers between devices  95.2 us (8%)
  between operations  16.3 us (1%)
    ppermute x55, waiting for transfers between devices, exchange(): return lax.ppermute(value, axis, [(a, a ^ bit) for a in range(size)])  392 us
    pallas_call x2, Pallas kernels, moe_back(): pl.pallas_call(lambda *refs: back_kernel(pieces, fs, len(big), tp_first,...  68.4 us
    ppermute x55, starting transfers between devices, exchange(): return lax.ppermute(value, axis, [(a, a ^ bit) for a in range(size)])  56.1 us
    pallas_call x3, Pallas kernels, whole_call(): pl.pallas_call(body, in_specs=[pl.BlockSpec(memory_space=pltpu.VMEM)] * l...  54 us
    pallas_call x1, Pallas kernels, moe_rows(): pl.pallas_call(lambda *refs: rows_kernel(pieces, fs, steps, groups, *refs...  47.3 us
    unnamed x172, local copies, waits for them, and re-layouts  46.3 us
    all_to_all x9, starting transfers between devices, turn(): return lax.all_to_all(value, 'fsdp', 0, 0)  38.6 us
    pallas_call x3, Pallas kernels, assemble(): pl.pallas_call(body, grid_spec=pltpu.PrefetchScalarGridSpec(num_scalar_pr...  37.5 us
  transfers between devices with their start and end apart: 71, of which 38 were waited for; matrix products, arithmetic and copies ran while one was open for 19% of the time, Pallas kernels for 16%

profile of v1, /device:TPU:0, one launch (start us, length us, event | category | flops | bytes accessed | tf_op | source)
XLA Modules:
  0.0 1130.2 jit_solution(7638549916870959186)
XLA Ops:
  15.9 19.2 %collective-permute-done = bf16[1,256,2048]{2,1,0:T(8,128)(2,1)} collective-permute-done((bf16[1,256,2048]{2,1,0:T(8,128)(2,1)S(1)}, bf16[1,256,2048]{2,1,0:T(8,128)(2,1)}, u32[]{:S(2)}, u32[]{:S(2)}) %collective-permute-start) | collective-permute-done | bytes 1048608 | tf_op jit(solution)/shard_map/ppermute | solution.py:87
  52.3 12.4 %all-gather.15.cloned.1.call-done = bf16[2176,512]{1,0:T(8,128)(2,1)} async-done(((bf16[544,512]{1,0:T(8,128)(2,1)}), bf16[2176,512]{1,0:T(8,128)(2,1)}) %all-gather.15.cloned.1.call-update) | async-done | bytes 2228240 | tf_op jit(solution)/shard_map/all_gather | solution.py:831
  74.4 5.3 fusion.2.refs_0_.normed
  79.7 7.9 collective-permute-done.2
  97.9 10.8 all-gather.17.cloned.1.call-done
  114.4 23.3 %attend.1 = (bf16[2,2,128,2048]{3,2,1,0:T(8,128)(2,1)}, bf16[2,2,128,2048]{3,2,1,0:T(8,128)(2,1)}, f32[1024,576]{1,0:T(8,128)}, bf16[1024,576]{1,0:T(8,128)(2,1)...) custom-call(bf16[1024,2048]{1,0:T(8,128)(2,1)} %fusion.2.refs_0_.nor, ...), custom_call_target="tpu_custom_call" | custom-call | bytes 1000000 | tf_op jit(solution)/shard_map/attend/pallas_call | solution.py:483
  145.1 4.5 add_convert_fusion.9
  149.6 24.9 %all-gather.19.cloned.1.call-done = bf16[512,2048]{1,0:T(8,128)(2,1)} async-done(((bf16[128,2048]{1,0:T(8,128)(2,1)}), bf16[512,2048]{1,0:T(8,128)(2,1)}) %all-gather.19.cloned.1.call-update) | async-done | bytes 2097168 | tf_op jit(solution)/shard_map/all_gather | solution.py:859
  177.5 22.9 %collective-permute-done.7 = bf16[1,2,128,2048]{3,2,1,0:T(8,128)(2,1)S(1)} collective-permute-done((bf16[1,2,128,2048]{3,2,1,0:T(8,128)(2,1)S(1)}, bf16[1,2,128,2048]{3,2,1,0:T(8,128)(2,1)S(1)}, u32[]{:S(2)}, u32[]{:S(2)}) %collective-permute-start.7) | collective-permute-done | bytes 1048608 | tf_op jit(solution)/shard_map/ppermute | solution.py:87
  202.5 10.7 collective-permute-done.8
  225.9 22.1 %collective-permute-done.9 = bf16[1,1,2,128,2048]{4,3,2,1,0:T(8,128)(2,1)S(1)} collective-permute-done((bf16[1,1,2,128,2048]{4,3,2,1,0:T(8,128)(2,1)S(1)}, bf16[1,1,2,128,2048]{4,3,2,1,0:T(8,128)(2,1)S(1)}, u32[]{:S(2)}, u32[]{:S(2)}) %collective-permute-start.9) | collective-permute-done | bytes 1048608 | tf_op jit(solution)/shard_map/ppermute | solution.py:87
  257.6 8.5 all-gather.21.cloned.1.call-done
  276.1 20.5 %collective-permute-done.10 = bf16[2,1,2,128,2048]{4,3,2,1,0:T(8,128)(2,1)} collective-permute-done((bf16[2,1,2,128,2048]{4,3,2,1,0:T(8,128)(2,1)}, bf16[2,1,2,128,2048]{4,3,2,1,0:T(8,128)(2,1)}, u32[]{:S(2)}, u32[]{:S(2)}) %collective-permute-start.10) | collective-permute-done | bytes 2097184 | tf_op jit(solution)/shard_map/ppermute | solution.py:87
  306.4 20.4 %collective-permute-done.13 = bf16[1,1,2,128,2048]{4,3,2,1,0:T(8,128)(2,1)S(1)} collective-permute-done((bf16[1,1,2,128,2048]{4,3,2,1,0:T(8,128)(2,1)S(1)}, bf16[1,1,2,128,2048]{4,3,2,1,0:T(8,128)(2,1)S(1)}, u32[]{:S(2)}, u32[]{:S(2)}) %collective-permute-start.13) | collective-permute-done | bytes 1048608 | tf_op jit(solution)/shard_map/ppermute | solution.py:87
  353.8 19.8 %collective-permute-done.14 = bf16[2,1,2,128,2048]{4,3,2,1,0:T(8,128)(2,1)} collective-permute-done((bf16[2,1,2,128,2048]{4,3,2,1,0:T(8,128)(2,1)}, bf16[2,1,2,128,2048]{4,3,2,1,0:T(8,128)(2,1)}, u32[]{:S(2)}, u32[]{:S(2)}) %collective-permute-start.14) | collective-permute-done | bytes 2097184 | tf_op jit(solution)/shard_map/ppermute | solution.py:87
  392.2 47.3 %moe_rows.1 = (bf16[2048,2048]{1,0:T(8,128)(2,1)}, bf16[2048,2048]{1,0:T(8,128)(2,1)}, f32[2048,704]{1,0:T(8,128)}, f32[2048,704]{1,0:T(8,128)}, bf16[4096,384]{1,0:T(8,128)(2,1)}, /*index=5*/f32[384,2048]{1,0:T(8,128)}) custom-call(s32[16,1,256]{2,1,0:T(1,128)} %reshape.364.refs_0_.refs_4_, bf16[384,2048]{1,0:T(8,128)(2,1)} %bitcast.206, ...), custom_call_target="tpu_custom_call" | custom-call | bytes 1000000 | tf_op jit(solution)/shard_map/moe_rows/pallas_call | solution.py:215
  439.5 7.3 all-to-all-done.3.refs_11_.refs_5_
  448.5 34.1 %moe_back.2 = (bf16[2048,704]{1,0:T(8,128)(2,1)}, bf16[2048,704]{1,0:T(8,128)(2,1)}, bf16[2048,704]{1,0:T(8,128)(2,1)}, bf16[2,2,2,128,2176]{4,3,2,1,0:T(8,128)(2,1)}, bf16[2,2,2,128,2176]{4,3,2,1,0:T(8,128)(2,1)}) custom-call(s32[1]{0:T(128)} %constant.211.clone.1.refs_0_, bf16[2048,2048]{1,0:T(8,128)(2,1)} %get-tuple-element.114.refs_1_.right_ref, ...), custom_call_target="tpu_custom_call" | custom-call | bytes 1000000 | tf_op jit(solution)/shard_map/moe_back/pallas_call | solution.py:333
  482.6 34.3 %moe_back.3 = (bf16[2048,704]{1,0:T(8,128)(2,1)}, bf16[2048,704]{1,0:T(8,128)(2,1)}, bf16[2048,704]{1,0:T(8,128)(2,1)}, bf16[2,2,2,128,2176]{4,3,2,1,0:T(8,128)(2,1)}, bf16[2,2,2,128,2176]{4,3,2,1,0:T(8,128)(2,1)}) custom-call(s32[1]{0:T(128)} %constant.211.clone.1.refs_0_, ...), custom_call_target="tpu_custom_call", output_to_operand_aliasing={{0}: (13, {}), {1}: (14, {}), {2}: (15, {})} | custom-call | bytes 1000000 | tf_op jit(solution)/shard_map/moe_back/pallas_call | solution.py:333
  517.4 7.2 collective-permute-done.22
  535.9 10.0 weight_grads.3
  548.9 15.6 %moe_out.3 = (bf16[2,2,2,128,2048]{4,3,2,1,0:T(8,128)(2,1)}, bf16[2,2,2,128,2048]{4,3,2,1,0:T(8,128)(2,1)}) custom-call(s32[1]{0:T(128)} %constant.211.clone.1.refs_0_, bf16[2048,704]{1,0:T(8,128)(2,1)S(1)} %copy-done.10, s32[16,256,1]{2,1,0:T(8,128)S(1)} %copy-done.6, bf16[4096,384]{1,0:T(8,128)(2,1)S(1)} %copy-done.8, bf16[384,2048]{1,0:T(8,128)(2,1)S(1)} %bitcast.209, ...), custom_call_target="tpu_custom_call" | custom-call | bytes 1000000 | tf_op jit(solution)/shard_map/moe_out/pallas_call | solution.py:412
  564.5 5.1 all-to-all-start.4
  576.3 15.6 %moe_out.2 = (bf16[2,2,2,128,2048]{4,3,2,1,0:T(8,128)(2,1)}, bf16[2,2,2,128,2048]{4,3,2,1,0:T(8,128)(2,1)}) custom-call(s32[1]{0:T(128)} %constant.211.clone.1.refs_0_, bf16[2048,704]{1,0:T(8,128)(2,1)S(1)} %copy-done.11, s32[16,256,1]{2,1,0:T(8,128)S(1)} %copy-done.7, bf16[4096,384]{1,0:T(8,128)(2,1)S(1)} %copy-done.9, bf16[384,2048]{1,0:T(8,128)(2,1)S(1)} %bitcast.210, ...), custom_call_target="tpu_custom_call" | custom-call | bytes 1000000 | tf_op jit(solution)/shard_map/moe_out/pallas_call | solution.py:412
  600.5 21.4 %collective-permute-done.27 = bf16[1,2,128,2176]{3,2,1,0:T(8,128)(2,1)S(1)} collective-permute-done((bf16[1,2,128,2176]{3,2,1,0:T(8,128)(2,1)S(1)}, bf16[1,2,128,2176]{3,2,1,0:T(8,128)(2,1)S(1)}, u32[]{:S(2)}, u32[]{:S(2)}) %collective-permute-start.27) | collective-permute-done | bytes 1114144 | tf_op jit(solution)/shard_map/ppermute | solution.py:87
  628.9 6.1 add_convert_fusion.2
  635.6 4.5 all-to-all-start.5
  651.3 10.5 weight_grads.4
  661.8 10.3 weight_grads.5
  672.1 19.0 %collective-permute-done.30 = bf16[1,2,2,128,2048]{4,3,2,1,0:T(8,128)(2,1)} collective-permute-done((bf16[1,2,2,128,2048]{4,3,2,1,0:T(8,128)(2,1)}, bf16[1,2,2,128,2048]{4,3,2,1,0:T(8,128)(2,1)}, u32[]{:S(2)}, u32[]{:S(2)}) %collective-permute-start.30) | collective-permute-done | bytes 2097184 | tf_op jit(solution)/shard_map/ppermute | solution.py:87
  706.2 11.4 %collective-permute-done.31 = bf16[1,1,128,2048]{3,2,1,0:T(8,128)(2,1)S(1)} collective-permute-done((bf16[1,1,128,2048]{3,2,1,0:T(8,128)(2,1)S(1)}, bf16[1,1,128,2048]{3,2,1,0:T(8,128)(2,1)S(1)}, u32[]{:S(2)}, u32[]{:S(2)}) %collective-permute-start.31) | collective-permute-done | bytes 524320 | tf_op jit(solution)/shard_map/ppermute | solution.py:87
  718.6 4.6 all-to-all-start.6
  724.1 22.1 %collective-permute-done.32 = bf16[2,1,128,2048]{3,2,1,0:T(8,128)(2,1)S(1)} collective-permute-done((bf16[2,1,128,2048]{3,2,1,0:T(8,128)(2,1)}, bf16[2,1,128,2048]{3,2,1,0:T(8,128)(2,1)S(1)}, u32[]{:S(2)}, u32[]{:S(2)}) %collective-permute-start.32) | collective-permute-done | bytes 1048608 | tf_op jit(solution)/shard_map/ppermute | solution.py:87
  746.5 4.4 collective-permute-done.33
  753.2 21.6 %attend_back.1 = (bf16[2,2,128,2688]{3,2,1,0:T(8,128)(2,1)}, bf16[2,2,128,2688]{3,2,1,0:T(8,128)(2,1)}, bf16[1024,384]{1,0:T(8,128)(2,1)}, bf16[1024,512]{1,0:T(8,128)(2,1)}) custom-call(bf16[1024,2048]{1,0:T(8,128)(2,1)} %bitcast.211, bf16[256,2048]{1,0:T(8,128)(2,1)} %bitcast.222, bf16[2,1024,1024]{2,1,0:T(8,128)(2,1)} %get-tuple-element.140.refs_2_, ...), custom_call_target="tpu_custom_call" | custom-call | bytes 1000000 | tf_op jit(solution)/shard_map/attend_back/pallas_call | solution.py:483
  774.9 11.5 %all-to-all-done.6 = bf16[4,704,512]{2,1,0:T(8,128)(2,1)} async-done(((bf16[4,704,512]{2,1,0:T(8,128)(2,1)}), bf16[4,704,512]{2,1,0:T(8,128)(2,1)}, u32[]{:S(2)}, u32[]{:S(2)}) %all-to-all-start.6) | async-done | bytes 2883616 | tf_op jit(solution)/shard_map/all_to_all | solution.py:794
  786.4 5.3 collective-permute-done.34
  796.7 4.8 all-to-all-start.8
  801.6 26.7 %collective-permute-done.35 = bf16[1,2,128,2688]{3,2,1,0:T(8,128)(2,1)} collective-permute-done((bf16[1,2,128,2688]{3,2,1,0:T(8,128)(2,1)S(1)}, bf16[1,2,128,2688]{3,2,1,0:T(8,128)(2,1)}, u32[]{:S(2)}, u32[]{:S(2)}) %collective-permute-start.35) | collective-permute-done | bytes 1376288 | tf_op jit(solution)/shard_map/ppermute | solution.py:87
  834.7 10.6 assemble.3
  848.4 9.0 attend_weights.1
  857.5 21.5 %collective-permute-done.36 = bf16[1,128,2688]{2,1,0:T(8,128)(2,1)} collective-permute-done((bf16[1,128,2688]{2,1,0:T(8,128)(2,1)}, bf16[1,128,2688]{2,1,0:T(8,128)(2,1)}, u32[]{:S(2)}, u32[]{:S(2)}) %collective-permute-start.36) | collective-permute-done | bytes 688160 | tf_op jit(solution)/shard_map/ppermute | solution.py:87
  891.0 6.2 collective-permute-done.40
  926.1 16.1 %collective-permute-done.38 = bf16[1,2,128,2048]{3,2,1,0:T(8,128)(2,1)S(1)} collective-permute-done((bf16[1,2,128,2048]{3,2,1,0:T(8,128)(2,1)S(1)}, bf16[1,2,128,2048]{3,2,1,0:T(8,128)(2,1)S(1)}, u32[]{:S(2)}, u32[]{:S(2)}) %collective-permute-start.38) | collective-permute-done | bytes 1048608 | tf_op jit(solution)/shard_map/ppermute | solution.py:87
  942.7 23.7 %collective-permute-done.37 = bf16[1,2,128,2048]{3,2,1,0:T(8,128)(2,1)S(1)} collective-permute-done((bf16[1,2,128,2048]{3,2,1,0:T(8,128)(2,1)S(1)}, bf16[1,2,128,2048]{3,2,1,0:T(8,128)(2,1)S(1)}, u32[]{:S(2)}, u32[]{:S(2)}) %collective-permute-start.37) | collective-permute-done | bytes 1048608 | tf_op jit(solution)/shard_map/ppermute | solution.py:87
  980.7 10.6 assemble.4
  1002.5 43.8 %collective-permute-done.48 = bf16[1,912,512]{2,1,0:T(8,128)(2,1)S(1)} collective-permute-done((bf16[1,912,512]{2,1,0:T(8,128)(2,1)S(1)}, bf16[1,912,512]{2,1,0:T(8,128)(2,1)S(1)}, u32[]{:S(2)}, u32[]{:S(2)}) %collective-permute-start.48) | collective-permute-done | bytes 933920 | tf_op jit(solution)/shard_map/ppermute | solution.py:87
  1106.6 16.3 %assemble.5 = f32[16,704,512]{2,1,0:T(8,128)} custom-call(s32[16]{0:T(128)S(1)} %iota.57.dest_ref, bf16[16,968,512]{2,1,0:T(8,128)(2,1)} %all-gather.27.cloned.1.call-done.refs_0_), custom_call_target="tpu_custom_call" | custom-call | bytes 36000000 | tf_op jit(solution)/shard_map/assemble/pallas_call | solution.py:665
  (499 shorter events, 362.3 us)
Async XLA Ops:
  7.3 57.4 %all-gather.15.cloned.1.call-start = ((), (), s32[]{:S(2)}) async-start(), calls=%async_computation.9 | async-start | bytes 2785280 | tf_op jit(solution)/shard_map/all_gather | solution.py:831
  8.8 26.3 %collective-permute-start = (bf16[1,256,2048]{2,1,0:T(8,128)(2,1)S(1)}, bf16[1,256,2048]{2,1,0:T(8,128)(2,1)}, u32[]{:S(2)}, u32[]{:S(2)}) collective-permute-start(bf16[1,256,2048]{2,1,0:T(8,128)(2,1)S(1)} %maximum_bitcast_fusion), channel_id=1, source_target_pairs={{0,4},{2,6},{4,0},{6,2},{1,5},{3,7},{5,1},{7,3},{8,12},{10,14},{12... | collective-permute-start | bytes 3145736 | tf_op jit(solution)/shard_map/ppermute | solution.py:87
  15.8 92.9 %all-gather.17.cloned.1.call-start = ((), (), s32[]{:S(2)}) async-start(), calls=%async_computation.10 | async-start | bytes 1966080 | tf_op jit(solution)/shard_map/all_gather | solution.py:847
  73.5 100.9 %all-gather.19.cloned.1.call-start = ((), (), s32[]{:S(2)}) async-start(), calls=%async_computation.11 | async-start | bytes 2621440 | tf_op jit(solution)/shard_map/all_gather | solution.py:859
  141.4 75.7 %all-to-all-start = ((bf16[4,704,512]{2,1,0:T(8,128)(2,1)}), bf16[4,704,512]{2,1,0:T(8,128)(2,1)S(1)}, u32[]{:S(2)}, u32[]{:S(2)}) async-start(bf16[4,704,512]{2,1,0:T(8,128)(2,1)} %dynamic-slice_bitcast_fusion.1), calls=%async_computation | async-start | bytes 5767168 | tf_op jit(solution)/shard_map/all_to_all | solution.py:794
  145.0 121.0 %all-gather.21.cloned.1.call-start = ((), (), s32[]{:S(2)}) async-start(), calls=%async_computation.12 | async-start | bytes 2621440 | tf_op jit(solution)/shard_map/all_gather | solution.py:910
  175.9 24.5 %collective-permute-start.7 = (bf16[1,2,128,2048]{3,2,1,0:T(8,128)(2,1)S(1)}, bf16[1,2,128,2048]{3,2,1,0:T(8,128)(2,1)S(1)}, u32[]{:S(2)}, u32[]{:S(2)}) collective-permute-start(bf16[1,2,128,2048]{3,2,1,0:T(8,128)(2,1)S(1)} %slice.256), channel_id=1, source_target_pairs={{0,1},{1,0},{2,3},{3,2},{4,5},{5,4},{6,7},{7,6},{8,9},{9,8},{10,11... | collective-permute-start | bytes 3145736 | tf_op jit(solution)/shard_map/ppermute | solution.py:87
  222.9 25.1 %collective-permute-start.9 = (bf16[1,1,2,128,2048]{4,3,2,1,0:T(8,128)(2,1)S(1)}, bf16[1,1,2,128,2048]{4,3,2,1,0:T(8,128)(2,1)S(1)}, u32[]{:S(2)}, u32[]{:S(2)}) collective-permute-start(bf16[1,1,2,128,2048]{4,3,2,1,0:T(8,128)(2,1)S(1)} %get-tuple-element.256), channel_id=1, source_target_pairs={{0,4},{2,6},{4,0},{6,2},{1,5},{3,7},{5,1},{7,3},{8,12},{10,14},{12... | collective-permute-start | bytes 3145736 | tf_op jit(solution)/shard_map/ppermute | solution.py:87
  224.5 26.5 %collective-permute-start.11 = (bf16[1,1,2,128,2048]{4,3,2,1,0:T(8,128)(2,1)S(1)}, bf16[1,1,2,128,2048]{4,3,2,1,0:T(8,128)(2,1)S(1)}, u32[]{:S(2)}, u32[]{:S(2)}) collective-permute-start(bf16[1,1,2,128,2048]{4,3,2,1,0:T(8,128)(2,1)S(1)} %get-tuple-element.255), channel_id=1, source_target_pairs={{0,1},{1,0},{2,3},{3,2},{4,5},{5,4},{6,7},{7,6},{8,9},{9,8},{10,11... | collective-permute-start | bytes 3145736 | tf_op jit(solution)/shard_map/ppermute | solution.py:87
  249.5 47.1 %collective-permute-start.10 = (bf16[2,1,2,128,2048]{4,3,2,1,0:T(8,128)(2,1)}, bf16[2,1,2,128,2048]{4,3,2,1,0:T(8,128)(2,1)}, u32[]{:S(2)}, u32[]{:S(2)}) collective-permute-start(bf16[2,1,2,128,2048]{4,3,2,1,0:T(8,128)(2,1)} %pad_maximum_fusion.7), channel_id=1, source_target_pairs={{0,1},{1,0},{2,3},{3,2},{4,5},{5,4},{6,7},{7,6},{8,9},{9,8},{10,11... | collective-permute-start | bytes 6291464 | tf_op jit(solution)/shard_map/ppermute | solution.py:87
  252.5 47.3 %collective-permute-start.12 = (bf16[1,2,2,128,2048]{4,3,2,1,0:T(8,128)(2,1)}, bf16[1,2,2,128,2048]{4,3,2,1,0:T(8,128)(2,1)}, u32[]{:S(2)}, u32[]{:S(2)}) collective-permute-start(bf16[1,2,2,128,2048]{4,3,2,1,0:T(8,128)(2,1)} %pad_maximum_fusion.8), channel_id=1, source_target_pairs={{0,4},{2,6},{4,0},{6,2},{1,5},{3,7},{5,1},{7,3},{8,12},{10,14},{12... | collective-permute-start | bytes 6291464 | tf_op jit(solution)/shard_map/ppermute | solution.py:87
  266.1 76.2 %all-to-all-start.1 = ((bf16[4,704,512]{2,1,0:T(8,128)(2,1)}), bf16[4,704,512]{2,1,0:T(8,128)(2,1)S(1)}, u32[]{:S(2)}, u32[]{:S(2)}) async-start(bf16[4,704,512]{2,1,0:T(8,128)(2,1)} %dynamic-slice_bitcast_fusion), calls=%async_computation.1 | async-start | bytes 5767168 | tf_op jit(solution)/shard_map/all_to_all | solution.py:794
  303.4 23.4 %collective-permute-start.13 = (bf16[1,1,2,128,2048]{4,3,2,1,0:T(8,128)(2,1)S(1)}, bf16[1,1,2,128,2048]{4,3,2,1,0:T(8,128)(2,1)S(1)}, u32[]{:S(2)}, u32[]{:S(2)}) collective-permute-start(bf16[1,1,2,128,2048]{4,3,2,1,0:T(8,128)(2,1)S(1)} %get-tuple-element.254), channel_id=1, source_target_pairs={{0,4},{2,6},{4,0},{6,2},{1,5},{3,7},{5,1},{7,3},{8,12},{10,14},{12... | collective-permute-start | bytes 3145736 | tf_op jit(solution)/shard_map/ppermute | solution.py:87
  304.9 25.0 %collective-permute-start.16 = (bf16[1,1,2,128,2048]{4,3,2,1,0:T(8,128)(2,1)S(1)}, bf16[1,1,2,128,2048]{4,3,2,1,0:T(8,128)(2,1)S(1)}, u32[]{:S(2)}, u32[]{:S(2)}) collective-permute-start(bf16[1,1,2,128,2048]{4,3,2,1,0:T(8,128)(2,1)S(1)} %get-tuple-element.253), channel_id=1, source_target_pairs={{0,1},{1,0},{2,3},{3,2},{4,5},{5,4},{6,7},{7,6},{8,9},{9,8},{10,11... | collective-permute-start | bytes 3145736 | tf_op jit(solution)/shard_map/ppermute | solution.py:87
  328.5 45.2 %collective-permute-start.14 = (bf16[2,1,2,128,2048]{4,3,2,1,0:T(8,128)(2,1)}, bf16[2,1,2,128,2048]{4,3,2,1,0:T(8,128)(2,1)}, u32[]{:S(2)}, u32[]{:S(2)}) collective-permute-start(bf16[2,1,2,128,2048]{4,3,2,1,0:T(8,128)(2,1)} %pad_maximum_fusion.9), channel_id=1, source_target_pairs={{0,1},{1,0},{2,3},{3,2},{4,5},{5,4},{6,7},{7,6},{8,9},{9,8},{10,11... | collective-permute-start | bytes 6291464 | tf_op jit(solution)/shard_map/ppermute | solution.py:87
  332.4 48.5 %collective-permute-start.17 = (bf16[1,2,2,128,2048]{4,3,2,1,0:T(8,128)(2,1)}, bf16[1,2,2,128,2048]{4,3,2,1,0:T(8,128)(2,1)}, u32[]{:S(2)}, u32[]{:S(2)}) collective-permute-start(bf16[1,2,2,128,2048]{4,3,2,1,0:T(8,128)(2,1)} %pad_maximum_fusion.10), channel_id=1, source_target_pairs={{0,4},{2,6},{4,0},{6,2},{1,5},{3,7},{5,1},{7,3},{8,12},{10,14},{12... | collective-permute-start | bytes 6291464 | tf_op jit(solution)/shard_map/ppermute | solution.py:87
  345.3 31.7 %all-to-all-start.2 = ((bf16[4,3,88,512]{3,2,1,0:T(8,128)(2,1)}), bf16[4,3,88,512]{3,2,1,0:T(8,128)(2,1)}, u32[]{:S(2)}, u32[]{:S(2)}) async-start(bf16[4,3,88,512]{3,2,1,0:T(8,128)(2,1)} %copy.147), calls=%async_computation.2 | async-start | bytes 2162688 | tf_op jit(solution)/shard_map/all_to_all | solution.py:794
  353.3 36.9 %collective-permute-start.19 = (bf16[2,2,2,128,2048]{4,3,2,1,0:T(8,128)(2,1)}, bf16[2,2,2,128,2048]{4,3,2,1,0:T(8,128)(2,1)}, u32[]{:S(2)}, u32[]{:S(2)}) collective-permute-start(bf16[2,2,2,128,2048]{4,3,2,1,0:T(8,128)(2,1)} %constant_dynamic-update-slice_fusion.6.refs_6_), channel_id=1, source_target_pairs={{0,2},{2,0},{4,6},{6,4},{1,3},{3,1},{5,7},{7,5},{8,10},{10,8},{12,... | collective-permute-start | bytes 12582920 | tf_op jit(solution)/shard_map/ppermute | solution.py:87
  353.3 36.9 %collective-permute-start.20 = (bf16[2,2,2,128,2048]{4,3,2,1,0:T(8,128)(2,1)}, bf16[2,2,2,128,2048]{4,3,2,1,0:T(8,128)(2,1)}, u32[]{:S(2)}, u32[]{:S(2)}) collective-permute-start(bf16[2,2,2,128,2048]{4,3,2,1,0:T(8,128)(2,1)} %constant_dynamic-update-slice_fusion.8.refs_8_), channel_id=1, source_target_pairs={{0,2},{2,0},{4,6},{6,4},{1,3},{3,1},{5,7},{7,5},{8,10},{10,8},{12,... | collective-permute-start | bytes 12582920 | tf_op jit(solution)/shard_map/ppermute | solution.py:87
  377.1 69.8 %all-to-all-start.3 = ((bf16[4,704,512]{2,1,0:T(8,128)(2,1)}), bf16[4,704,512]{2,1,0:T(8,128)(2,1)S(1)}, u32[]{:S(2)}, u32[]{:S(2)}) async-start(bf16[4,704,512]{2,1,0:T(8,128)(2,1)} %constant_dynamic-slice_fusion), calls=%async_computation.3 | async-start | bytes 5767168 | tf_op jit(solution)/shard_map/all_to_all | solution.py:794
  530.0 62.5 %collective-permute-start.26 = (bf16[1,2,2,128,2176]{4,3,2,1,0:T(8,128)(2,1)}, bf16[1,2,2,128,2176]{4,3,2,1,0:T(8,128)(2,1)}, u32[]{:S(2)}, u32[]{:S(2)}) collective-permute-start(bf16[1,2,2,128,2176]{4,3,2,1,0:T(8,128)(2,1)} %slice.329), channel_id=1, source_target_pairs={{0,4},{2,6},{4,0},{6,2},{1,5},{3,7},{5,1},{7,3},{8,12},{10,14},{12... | collective-permute-start | bytes 6684680 | tf_op jit(solution)/shard_map/ppermute | solution.py:87
  534.4 62.1 %collective-permute-start.24 = (bf16[1,2,2,128,2176]{4,3,2,1,0:T(8,128)(2,1)}, bf16[1,2,2,128,2176]{4,3,2,1,0:T(8,128)(2,1)}, u32[]{:S(2)}, u32[]{:S(2)}) collective-permute-start(bf16[1,2,2,128,2176]{4,3,2,1,0:T(8,128)(2,1)} %slice.327), channel_id=1, source_target_pairs={{0,1},{1,0},{2,3},{3,2},{4,5},{5,4},{6,7},{7,6},{8,9},{9,8},{10,11... | collective-permute-start | bytes 6684680 | tf_op jit(solution)/shard_map/ppermute | solution.py:87
  564.5 63.0 %collective-permute-start.29 = (bf16[2,2,2,128,2048]{4,3,2,1,0:T(8,128)(2,1)}, bf16[2,2,2,128,2048]{4,3,2,1,0:T(8,128)(2,1)}, u32[]{:S(2)}, u32[]{:S(2)}) collective-permute-start(bf16[2,2,2,128,2048]{4,3,2,1,0:T(8,128)(2,1)} %get-tuple-element.129), channel_id=1, source_target_pairs={{0,2},{2,0},{4,6},{6,4},{1,3},{3,1},{5,7},{7,5},{8,10},{10,8},{12,... | collective-permute-start | bytes 12582920 | tf_op jit(solution)/shard_map/ppermute | solution.py:87
  564.5 71.1 %all-to-all-start.4 = ((bf16[4,704,512]{2,1,0:T(8,128)(2,1)}), bf16[4,704,512]{2,1,0:T(8,128)(2,1)}, u32[]{:S(2)}, u32[]{:S(2)}) async-start(bf16[4,704,512]{2,1,0:T(8,128)(2,1)} %copy-done.13), calls=%async_computation.4 | async-start | bytes 5767168 | tf_op jit(solution)/shard_map/all_to_all | solution.py:794
  592.0 52.7 %collective-permute-start.23 = (bf16[2,2,2,128,2048]{4,3,2,1,0:T(8,128)(2,1)}, bf16[2,2,2,128,2048]{4,3,2,1,0:T(8,128)(2,1)}, u32[]{:S(2)}, u32[]{:S(2)}) collective-permute-start(bf16[2,2,2,128,2048]{4,3,2,1,0:T(8,128)(2,1)} %get-tuple-element.127), channel_id=1, source_target_pairs={{0,2},{2,0},{4,6},{6,4},{1,3},{3,1},{5,7},{7,5},{8,10},{10,8},{12,... | collective-permute-start | bytes 12582920 | tf_op jit(solution)/shard_map/ppermute | solution.py:87
  595.4 26.5 %collective-permute-start.27 = (bf16[1,2,128,2176]{3,2,1,0:T(8,128)(2,1)S(1)}, bf16[1,2,128,2176]{3,2,1,0:T(8,128)(2,1)S(1)}, u32[]{:S(2)}, u32[]{:S(2)}) collective-permute-start(bf16[1,2,128,2176]{3,2,1,0:T(8,128)(2,1)S(1)} %slice.271), channel_id=1, source_target_pairs={{0,1},{1,0},{2,3},{3,2},{4,5},{5,4},{6,7},{7,6},{8,9},{9,8},{10,11... | collective-permute-start | bytes 3342344 | tf_op jit(solution)/shard_map/ppermute | solution.py:87
  599.4 26.3 %collective-permute-start.25 = (bf16[1,2,128,2176]{3,2,1,0:T(8,128)(2,1)S(1)}, bf16[1,2,128,2176]{3,2,1,0:T(8,128)(2,1)S(1)}, u32[]{:S(2)}, u32[]{:S(2)}) collective-permute-start(bf16[1,2,128,2176]{3,2,1,0:T(8,128)(2,1)S(1)} %slice.267), channel_id=1, source_target_pairs={{0,4},{2,6},{4,0},{6,2},{1,5},{3,7},{5,1},{7,3},{8,12},{10,14},{12... | collective-permute-start | bytes 3342344 | tf_op jit(solution)/shard_map/ppermute | solution.py:87
  635.6 65.7 %all-to-all-start.5 = ((bf16[4,128,2176]{2,1,0:T(8,128)(2,1)}), bf16[4,128,2176]{2,1,0:T(8,128)(2,1)}, u32[]{:S(2)}, u32[]{:S(2)}) async-start(bf16[4,128,2176]{2,1,0:T(8,128)(2,1)} %pad_maximum_fusion.5), calls=%async_computation.5 | async-start | bytes 4456448 | tf_op jit(solution)/shard_map/all_to_all | solution.py:794
  640.1 190.2 %all-gather.23.cloned.1.call-start = ((), (), s32[]{:S(2)}) async-start(), calls=%async_computation.13 | async-start | bytes 14417920 | tf_op jit(solution)/shard_map/all_gather | solution.py:1004
  643.5 47.6 %collective-permute-start.30 = (bf16[1,2,2,128,2048]{4,3,2,1,0:T(8,128)(2,1)}, bf16[1,2,2,128,2048]{4,3,2,1,0:T(8,128)(2,1)}, u32[]{:S(2)}, u32[]{:S(2)}) collective-permute-start(bf16[1,2,2,128,2048]{4,3,2,1,0:T(8,128)(2,1)} %slice.275), channel_id=1, source_target_pairs={{0,4},{2,6},{4,0},{6,2},{1,5},{3,7},{5,1},{7,3},{8,12},{10,14},{12... | collective-permute-start | bytes 6291464 | tf_op jit(solution)/shard_map/ppermute | solution.py:87
  650.3 47.2 %collective-permute-start.28 = (bf16[1,2,2,128,2048]{4,3,2,1,0:T(8,128)(2,1)}, bf16[1,2,2,128,2048]{4,3,2,1,0:T(8,128)(2,1)}, u32[]{:S(2)}, u32[]{:S(2)}) collective-permute-start(bf16[1,2,2,128,2048]{4,3,2,1,0:T(8,128)(2,1)} %slice.273), channel_id=1, source_target_pairs={{0,1},{1,0},{2,3},{3,2},{4,5},{5,4},{6,7},{7,6},{8,9},{9,8},{10,11... | collective-permute-start | bytes 6291464 | tf_op jit(solution)/shard_map/ppermute | solution.py:87
  718.6 67.7 %all-to-all-start.6 = ((bf16[4,704,512]{2,1,0:T(8,128)(2,1)}), bf16[4,704,512]{2,1,0:T(8,128)(2,1)}, u32[]{:S(2)}, u32[]{:S(2)}) async-start(bf16[4,704,512]{2,1,0:T(8,128)(2,1)} %weight_grads.4), calls=%async_computation.6 | async-start | bytes 5767168 | tf_op jit(solution)/shard_map/all_to_all | solution.py:794
  723.2 253.2 %all-gather.25.cloned.1.call-start = ((), (), s32[]{:S(2)}) async-start(), calls=%async_computation.14 | async-start | bytes 14417920 | tf_op jit(solution)/shard_map/all_gather | solution.py:1024
  723.3 22.9 %collective-permute-start.32 = (bf16[2,1,128,2048]{3,2,1,0:T(8,128)(2,1)}, bf16[2,1,128,2048]{3,2,1,0:T(8,128)(2,1)S(1)}, u32[]{:S(2)}, u32[]{:S(2)}) collective-permute-start(bf16[2,1,128,2048]{3,2,1,0:T(8,128)(2,1)} %pad_maximum_fusion.16), channel_id=1, source_target_pairs={{0,1},{1,0},{2,3},{3,2},{4,5},{5,4},{6,7},{7,6},{8,9},{9,8},{10,11... | collective-permute-start | bytes 3145736 | tf_op jit(solution)/shard_map/ppermute | solution.py:87
  795.8 32.4 %collective-permute-start.35 = (bf16[1,2,128,2688]{3,2,1,0:T(8,128)(2,1)S(1)}, bf16[1,2,128,2688]{3,2,1,0:T(8,128)(2,1)}, u32[]{:S(2)}, u32[]{:S(2)}) collective-permute-start(bf16[1,2,128,2688]{3,2,1,0:T(8,128)(2,1)S(1)} %slice.278), channel_id=1, source_target_pairs={{0,1},{1,0},{2,3},{3,2},{4,5},{5,4},{6,7},{7,6},{8,9},{9,8},{10,11... | collective-permute-start | bytes 4128776 | tf_op jit(solution)/shard_map/ppermute | solution.py:87
  796.7 109.5 %all-to-all-start.8 = ((bf16[4,968,512]{2,1,0:T(8,128)(2,1)}), bf16[4,968,512]{2,1,0:T(8,128)(2,1)}, u32[]{:S(2)}, u32[]{:S(2)}) async-start(bf16[4,968,512]{2,1,0:T(8,128)(2,1)} %weight_grads.5), calls=%async_computation.8 | async-start | bytes 7929856 | tf_op jit(solution)/shard_map/all_to_all | solution.py:794
  801.5 292.2 %all-gather.27.cloned.1.call-start = ((), (), s32[]{:S(2)}) async-start(), calls=%async_computation.15 | async-start | bytes 19824640 | tf_op jit(solution)/shard_map/all_gather | solution.py:1061
  846.2 32.8 %collective-permute-start.36 = (bf16[1,128,2688]{2,1,0:T(8,128)(2,1)}, bf16[1,128,2688]{2,1,0:T(8,128)(2,1)}, u32[]{:S(2)}, u32[]{:S(2)}) collective-permute-start(bf16[1,128,2688]{2,1,0:T(8,128)(2,1)} %slice.280), channel_id=1, source_target_pairs={{0,4},{2,6},{4,0},{6,2},{1,5},{3,7},{5,1},{7,3},{8,12},{10,14},{12... | collective-permute-start | bytes 2064392 | tf_op jit(solution)/shard_map/ppermute | solution.py:87
  916.1 26.1 %collective-permute-start.38 = (bf16[1,2,128,2048]{3,2,1,0:T(8,128)(2,1)S(1)}, bf16[1,2,128,2048]{3,2,1,0:T(8,128)(2,1)S(1)}, u32[]{:S(2)}, u32[]{:S(2)}) collective-permute-start(bf16[1,2,128,2048]{3,2,1,0:T(8,128)(2,1)S(1)} %slice.284), channel_id=1, source_target_pairs={{0,1},{1,0},{2,3},{3,2},{4,5},{5,4},{6,7},{7,6},{8,9},{9,8},{10,11... | collective-permute-start | bytes 3145736 | tf_op jit(solution)/shard_map/ppermute | solution.py:87
  918.5 47.9 %collective-permute-start.37 = (bf16[1,2,128,2048]{3,2,1,0:T(8,128)(2,1)S(1)}, bf16[1,2,128,2048]{3,2,1,0:T(8,128)(2,1)S(1)}, u32[]{:S(2)}, u32[]{:S(2)}) collective-permute-start(bf16[1,2,128,2048]{3,2,1,0:T(8,128)(2,1)S(1)} %slice.282), channel_id=1, source_target_pairs={{0,4},{2,6},{4,0},{6,2},{1,5},{3,7},{5,1},{7,3},{8,12},{10,14},{12... | collective-permute-start | bytes 3145736 | tf_op jit(solution)/shard_map/ppermute | solution.py:87
  921.4 45.6 %collective-permute-start.42 = (bf16[2,912,512]{2,1,0:T(8,128)(2,1)S(1)}, bf16[2,912,512]{2,1,0:T(8,128)(2,1)S(1)}, u32[]{:S(2)}, u32[]{:S(2)}) collective-permute-start(bf16[2,912,512]{2,1,0:T(8,128)(2,1)S(1)} %dynamic-slice_bitcast_fusion.2), channel_id=1, source_target_pairs={{0,8},{8,0},{16,24},{24,16},{1,9},{9,1},{17,25},{25,17},{2,10},{10... | collective-permute-start | bytes 5603336 | tf_op jit(solution)/shard_map/ppermute | solution.py:87
  924.8 49.1 %collective-permute-start.46 = (bf16[1,1,128,2048]{3,2,1,0:T(8,128)(2,1)}, bf16[1,1,128,2048]{3,2,1,0:T(8,128)(2,1)}, u32[]{:S(2)}, u32[]{:S(2)}) collective-permute-start(bf16[1,1,128,2048]{3,2,1,0:T(8,128)(2,1)} %fusion.29), channel_id=1, source_target_pairs={{0,1},{1,0},{2,3},{3,2},{4,5},{5,4},{6,7},{7,6},{8,9},{9,8},{10,11... | collective-permute-start | bytes 1572872 | tf_op jit(solution)/shard_map/ppermute | solution.py:87
  970.5 26.7 %collective-permute-start.43 = (bf16[2,128,2048]{2,1,0:T(8,128)(2,1)}, bf16[2,128,2048]{2,1,0:T(8,128)(2,1)}, u32[]{:S(2)}, u32[]{:S(2)}) collective-permute-start(bf16[2,128,2048]{2,1,0:T(8,128)(2,1)} %dynamic-slice_bitcast_fusion.3), channel_id=1, source_target_pairs={{0,8},{8,0},{16,24},{24,16},{1,9},{9,1},{17,25},{25,17},{2,10},{10... | collective-permute-start | bytes 3145736 | tf_op jit(solution)/shard_map/ppermute | solution.py:87
  991.5 54.9 %collective-permute-start.48 = (bf16[1,912,512]{2,1,0:T(8,128)(2,1)S(1)}, bf16[1,912,512]{2,1,0:T(8,128)(2,1)S(1)}, u32[]{:S(2)}, u32[]{:S(2)}) collective-permute-start(bf16[1,912,512]{2,1,0:T(8,128)(2,1)S(1)} %dynamic-slice_convert_fusion), channel_id=1, source_target_pairs={{0,16},{8,24},{16,0},{24,8},{1,17},{9,25},{17,1},{25,9},{2,18},{10... | collective-permute-start | bytes 2801672 | tf_op jit(solution)/shard_map/ppermute | solution.py:87
  999.7 69.2 %collective-permute-start.44 = (bf16[1,128,2048]{2,1,0:T(8,128)(2,1)}, bf16[1,128,2048]{2,1,0:T(8,128)(2,1)}, u32[]{:S(2)}, u32[]{:S(2)}) collective-permute-start(bf16[1,128,2048]{2,1,0:T(8,128)(2,1)} %dynamic-slice_convert_fusion.1), channel_id=1, source_target_pairs={{0,16},{8,24},{16,0},{24,8},{1,17},{9,25},{17,1},{25,9},{2,18},{10... | collective-permute-start | bytes 1572872 | tf_op jit(solution)/shard_map/ppermute | solution.py:87
  1046.7 25.1 %collective-permute-start.52 = (bf16[912,512]{1,0:T(8,128)(2,1)S(1)}, bf16[912,512]{1,0:T(8,128)(2,1)}, u32[]{:S(2)}, u32[]{:S(2)}) collective-permute-start(bf16[912,512]{1,0:T(8,128)(2,1)S(1)} %add_bitcast_fusion), channel_id=1, source_target_pairs={{0,4},{2,6},{4,0},{6,2},{1,5},{3,7},{5,1},{7,3},{8,12},{10,14},{12... | collective-permute-start | bytes 2801672 | tf_op jit(solution)/shard_map/ppermute | solution.py:87
  1047.3 25.8 %collective-permute-start.53 = (bf16[912,512]{1,0:T(8,128)(2,1)S(1)}, bf16[912,512]{1,0:T(8,128)(2,1)}, u32[]{:S(2)}, u32[]{:S(2)}) collective-permute-start(bf16[912,512]{1,0:T(8,128)(2,1)S(1)} %add_bitcast_fusion), channel_id=1, source_target_pairs={{0,2},{2,0},{4,6},{6,4},{1,3},{3,1},{5,7},{7,5},{8,10},{10,8},{12,... | collective-permute-start | bytes 2801672 | tf_op jit(solution)/shard_map/ppermute | solution.py:87
  1070.2 16.4 %collective-permute-start.45 = (bf16[1,1,128,2048]{3,2,1,0:T(8,128)(2,1)S(1)}, bf16[1,1,128,2048]{3,2,1,0:T(8,128)(2,1)}, u32[]{:S(2)}, u32[]{:S(2)}) collective-permute-start(bf16[1,1,128,2048]{3,2,1,0:T(8,128)(2,1)S(1)} %fusion.28), channel_id=1, source_target_pairs={{0,1},{1,0},{2,3},{3,2},{4,5},{5,4},{6,7},{7,6},{8,9},{9,8},{10,11... | collective-permute-start | bytes 1572872 | tf_op jit(solution)/shard_map/ppermute | solution.py:87
  (104 other events, 1139.8 us)
Sparse Core Ops, SparseCore 0:
  16.0 48.6 all-gather.14
  73.6 35.0 all-gather.16
  110.8 63.5 all-gather.18
  221.4 44.6 all-gather.20
  718.7 75.9 all-gather.22
  796.2 90.8 all-gather.24
  906.3 123.8 all-gather.26

commit v2 on v1

--- a/solution.py
+++ b/solution.py
@@ -1057,7 +1057,7 @@
     out_sum = hops(after(out_home, pack_sum), bits[:1])
     pack_sum = after(pack_sum, up_shards)
     pack_total = hops(pack_sum, bits[1:])[0]
-    out_total = hops(out_sum, bits[1:])[0]
+    out_total = hops(after(out_sum, pack_total), bits[1:])[0]
     down_blocks = lax.all_gather(after(down_back, d_w_latent), "ctx", axis=0)
     grad_x_norm, d_gain_attn = norm_back(x_rel, attn_scale[:n], gain_norm, grad_normed)
     input_own = (grad_mid + grad_x_norm).astype(bf16)
@@ -1074,6 +1074,7 @@
     )
 
     blocks = over_ctx(pack_total.astype(bf16))
+    gain_pin = blocks[1]
     at_q, at_e = hd * VHEAD, hd * VHEAD + q_cols
     by_group = [(j ^ m) // share for m in members]
     w_out_grad = place(
@@ -1107,7 +1108,7 @@
         ],
         axis=1,
     )
-    gain_sum = jnp.sum(turn(after(gain_parts[:, None, :], pack_total)), axis=0)
+    gain_sum = jnp.sum(turn(after(gain_parts[:, None, :], gain_pin)), axis=0)
     for bit in low_bits(tp):
         gain_sum = gain_sum + exchange(gain_sum, "tp", bit)
     for bit in low_bits(cx):

time: 1140 us -> 1140 us (level)
    unnamed x172 -> x164, local copies, waits for them, and re-layouts: 46.3 us -> 45.5 us
where the time goes in v2:
time: 1140 us; the launch traced here: 1130 us
  waiting for transfers between devices  480 us (42%)
  Pallas kernels  269 us (24%)
  local copies, waits for them, and re-layouts  136 us (12%)
  other arithmetic  134 us (12%)
  starting transfers between devices  90.8 us (8%)
  between operations  16.3 us (1%)
    ppermute x55, waiting for transfers between devices, exchange(): return lax.ppermute(value, axis, [(a, a ^ bit) for a in range(size)])  401 us
    pallas_call x2, Pallas kernels, moe_back(): pl.pallas_call(lambda *refs: back_kernel(pieces, fs, len(big), tp_first,...  68.4 us
    pallas_call x3, Pallas kernels, whole_call(): pl.pallas_call(body, in_specs=[pl.BlockSpec(memory_space=pltpu.VMEM)] * l...  54 us
    ppermute x55, starting transfers between devices, exchange(): return lax.ppermute(value, axis, [(a, a ^ bit) for a in range(size)])  52.6 us
    pallas_call x1, Pallas kernels, moe_rows(): pl.pallas_call(lambda *refs: rows_kernel(pieces, fs, steps, groups, *refs...  47.3 us
    unnamed x164, local copies, waits for them, and re-layouts  45.5 us
    pallas_call x3, Pallas kernels, assemble(): pl.pallas_call(body, grid_spec=pltpu.PrefetchScalarGridSpec(num_scalar_pr...  37.7 us
    all_to_all x9, starting transfers between devices, turn(): return lax.all_to_all(value, 'fsdp', 0, 0)  37.7 us
  transfers between devices with their start and end apart: 71, of which 38 were waited for; matrix products, arithmetic and copies ran while one was open for 19% of the time, Pallas kernels for 16%

profile of v2, /device:TPU:0, one launch (start us, length us, event | category | flops | bytes accessed | tf_op | source)
XLA Modules:
  0.0 1131.4 jit_solution(7746118969735984453)
XLA Ops:
  15.9 19.2 %collective-permute-done = bf16[1,256,2048]{2,1,0:T(8,128)(2,1)} collective-permute-done((bf16[1,256,2048]{2,1,0:T(8,128)(2,1)S(1)}, bf16[1,256,2048]{2,1,0:T(8,128)(2,1)}, u32[]{:S(2)}, u32[]{:S(2)}) %collective-permute-start) | collective-permute-done | bytes 1048608 | tf_op jit(solution)/shard_map/ppermute | solution.py:87
  52.2 12.4 %all-gather.15.cloned.1.call-done = bf16[2176,512]{1,0:T(8,128)(2,1)} async-done(((bf16[544,512]{1,0:T(8,128)(2,1)}), bf16[2176,512]{1,0:T(8,128)(2,1)}) %all-gather.15.cloned.1.call-update) | async-done | bytes 2228240 | tf_op jit(solution)/shard_map/all_gather | solution.py:831
  74.4 5.3 fusion.2.refs_0_.normed
  79.7 7.9 collective-permute-done.2
  97.9 10.8 all-gather.17.cloned.1.call-done
  114.4 23.3 %attend.1 = (bf16[2,2,128,2048]{3,2,1,0:T(8,128)(2,1)}, bf16[2,2,128,2048]{3,2,1,0:T(8,128)(2,1)}, f32[1024,576]{1,0:T(8,128)}, bf16[1024,576]{1,0:T(8,128)(2,1)...) custom-call(bf16[1024,2048]{1,0:T(8,128)(2,1)} %fusion.2.refs_0_.nor, ...), custom_call_target="tpu_custom_call" | custom-call | bytes 1000000 | tf_op jit(solution)/shard_map/attend/pallas_call | solution.py:483
  149.6 24.9 %all-gather.19.cloned.1.call-done = bf16[512,2048]{1,0:T(8,128)(2,1)} async-done(((bf16[128,2048]{1,0:T(8,128)(2,1)}), bf16[512,2048]{1,0:T(8,128)(2,1)}) %all-gather.19.cloned.1.call-update) | async-done | bytes 2097168 | tf_op jit(solution)/shard_map/all_gather | solution.py:859
  177.6 22.9 %collective-permute-done.7 = bf16[1,2,128,2048]{3,2,1,0:T(8,128)(2,1)S(1)} collective-permute-done((bf16[1,2,128,2048]{3,2,1,0:T(8,128)(2,1)S(1)}, bf16[1,2,128,2048]{3,2,1,0:T(8,128)(2,1)S(1)}, u32[]{:S(2)}, u32[]{:S(2)}) %collective-permute-start.7) | collective-permute-done | bytes 1048608 | tf_op jit(solution)/shard_map/ppermute | solution.py:87
  202.5 10.7 collective-permute-done.8
  226.0 22.1 %collective-permute-done.9 = bf16[1,1,2,128,2048]{4,3,2,1,0:T(8,128)(2,1)S(1)} collective-permute-done((bf16[1,1,2,128,2048]{4,3,2,1,0:T(8,128)(2,1)S(1)}, bf16[1,1,2,128,2048]{4,3,2,1,0:T(8,128)(2,1)S(1)}, u32[]{:S(2)}, u32[]{:S(2)}) %collective-permute-start.9) | collective-permute-done | bytes 1048608 | tf_op jit(solution)/shard_map/ppermute | solution.py:87
  257.6 8.5 all-gather.21.cloned.1.call-done
  276.1 20.5 %collective-permute-done.10 = bf16[2,1,2,128,2048]{4,3,2,1,0:T(8,128)(2,1)} collective-permute-done((bf16[2,1,2,128,2048]{4,3,2,1,0:T(8,128)(2,1)}, bf16[2,1,2,128,2048]{4,3,2,1,0:T(8,128)(2,1)}, u32[]{:S(2)}, u32[]{:S(2)}) %collective-permute-start.10) | collective-permute-done | bytes 2097184 | tf_op jit(solution)/shard_map/ppermute | solution.py:87
  306.4 20.4 %collective-permute-done.13 = bf16[1,1,2,128,2048]{4,3,2,1,0:T(8,128)(2,1)S(1)} collective-permute-done((bf16[1,1,2,128,2048]{4,3,2,1,0:T(8,128)(2,1)S(1)}, bf16[1,1,2,128,2048]{4,3,2,1,0:T(8,128)(2,1)S(1)}, u32[]{:S(2)}, u32[]{:S(2)}) %collective-permute-start.13) | collective-permute-done | bytes 1048608 | tf_op jit(solution)/shard_map/ppermute | solution.py:87
  353.8 19.9 %collective-permute-done.14 = bf16[2,1,2,128,2048]{4,3,2,1,0:T(8,128)(2,1)} collective-permute-done((bf16[2,1,2,128,2048]{4,3,2,1,0:T(8,128)(2,1)}, bf16[2,1,2,128,2048]{4,3,2,1,0:T(8,128)(2,1)}, u32[]{:S(2)}, u32[]{:S(2)}) %collective-permute-start.14) | collective-permute-done | bytes 2097184 | tf_op jit(solution)/shard_map/ppermute | solution.py:87
  392.3 47.3 %moe_rows.1 = (bf16[2048,2048]{1,0:T(8,128)(2,1)}, bf16[2048,2048]{1,0:T(8,128)(2,1)}, f32[2048,704]{1,0:T(8,128)}, f32[2048,704]{1,0:T(8,128)}, bf16[4096,384]{1,0:T(8,128)(2,1)}, /*index=5*/f32[384,2048]{1,0:T(8,128)}) custom-call(s32[16,1,256]{2,1,0:T(1,128)} %reshape.364.refs_0_.refs_4_, bf16[384,2048]{1,0:T(8,128)(2,1)} %bitcast.206, ...), custom_call_target="tpu_custom_call" | custom-call | bytes 1000000 | tf_op jit(solution)/shard_map/moe_rows/pallas_call | solution.py:215
  439.6 7.3 all-to-all-done.3.refs_11_.refs_5_
  448.5 34.1 %moe_back.2 = (bf16[2048,704]{1,0:T(8,128)(2,1)}, bf16[2048,704]{1,0:T(8,128)(2,1)}, bf16[2048,704]{1,0:T(8,128)(2,1)}, bf16[2,2,2,128,2176]{4,3,2,1,0:T(8,128)(2,1)}, bf16[2,2,2,128,2176]{4,3,2,1,0:T(8,128)(2,1)}) custom-call(s32[1]{0:T(128)} %constant.211.clone.1.refs_0_, bf16[2048,2048]{1,0:T(8,128)(2,1)} %get-tuple-element.115.refs_1_.right_ref, ...), custom_call_target="tpu_custom_call" | custom-call | bytes 1000000 | tf_op jit(solution)/shard_map/moe_back/pallas_call | solution.py:333
  482.6 34.3 %moe_back.3 = (bf16[2048,704]{1,0:T(8,128)(2,1)}, bf16[2048,704]{1,0:T(8,128)(2,1)}, bf16[2048,704]{1,0:T(8,128)(2,1)}, bf16[2,2,2,128,2176]{4,3,2,1,0:T(8,128)(2,1)}, bf16[2,2,2,128,2176]{4,3,2,1,0:T(8,128)(2,1)}) custom-call(s32[1]{0:T(128)} %constant.211.clone.1.refs_0_, ...), custom_call_target="tpu_custom_call", output_to_operand_aliasing={{0}: (13, {}), {1}: (14, {}), {2}: (15, {})} | custom-call | bytes 1000000 | tf_op jit(solution)/shard_map/moe_back/pallas_call | solution.py:333
  517.5 7.2 collective-permute-done.22
  536.0 10.0 weight_grads.3
  549.0 15.6 %moe_out.3 = (bf16[2,2,2,128,2048]{4,3,2,1,0:T(8,128)(2,1)}, bf16[2,2,2,128,2048]{4,3,2,1,0:T(8,128)(2,1)}) custom-call(s32[1]{0:T(128)} %constant.211.clone.1.refs_0_, bf16[2048,704]{1,0:T(8,128)(2,1)S(1)} %copy-done.10, s32[16,256,1]{2,1,0:T(8,128)S(1)} %copy-done.6, bf16[4096,384]{1,0:T(8,128)(2,1)S(1)} %copy-done.8, bf16[384,2048]{1,0:T(8,128)(2,1)S(1)} %bitcast.209, ...), custom_call_target="tpu_custom_call" | custom-call | bytes 1000000 | tf_op jit(solution)/shard_map/moe_out/pallas_call | solution.py:412
  564.6 5.1 all-to-all-start.4
  576.4 15.6 %moe_out.2 = (bf16[2,2,2,128,2048]{4,3,2,1,0:T(8,128)(2,1)}, bf16[2,2,2,128,2048]{4,3,2,1,0:T(8,128)(2,1)}) custom-call(s32[1]{0:T(128)} %constant.211.clone.1.refs_0_, bf16[2048,704]{1,0:T(8,128)(2,1)S(1)} %copy-done.11, s32[16,256,1]{2,1,0:T(8,128)S(1)} %copy-done.7, bf16[4096,384]{1,0:T(8,128)(2,1)S(1)} %copy-done.9, bf16[384,2048]{1,0:T(8,128)(2,1)S(1)} %bitcast.210, ...), custom_call_target="tpu_custom_call" | custom-call | bytes 1000000 | tf_op jit(solution)/shard_map/moe_out/pallas_call | solution.py:412
  600.6 21.4 %collective-permute-done.27 = bf16[1,2,128,2176]{3,2,1,0:T(8,128)(2,1)S(1)} collective-permute-done((bf16[1,2,128,2176]{3,2,1,0:T(8,128)(2,1)S(1)}, bf16[1,2,128,2176]{3,2,1,0:T(8,128)(2,1)S(1)}, u32[]{:S(2)}, u32[]{:S(2)}) %collective-permute-start.27) | collective-permute-done | bytes 1114144 | tf_op jit(solution)/shard_map/ppermute | solution.py:87
  629.0 6.1 add_convert_fusion.2
  635.7 4.5 all-to-all-start.5
  651.4 10.5 weight_grads.4
  661.9 10.3 weight_grads.5
  672.2 18.9 %collective-permute-done.30 = bf16[1,2,2,128,2048]{4,3,2,1,0:T(8,128)(2,1)} collective-permute-done((bf16[1,2,2,128,2048]{4,3,2,1,0:T(8,128)(2,1)}, bf16[1,2,2,128,2048]{4,3,2,1,0:T(8,128)(2,1)}, u32[]{:S(2)}, u32[]{:S(2)}) %collective-permute-start.30) | collective-permute-done | bytes 2097184 | tf_op jit(solution)/shard_map/ppermute | solution.py:87
  706.3 11.4 %collective-permute-done.31 = bf16[1,1,128,2048]{3,2,1,0:T(8,128)(2,1)S(1)} collective-permute-done((bf16[1,1,128,2048]{3,2,1,0:T(8,128)(2,1)S(1)}, bf16[1,1,128,2048]{3,2,1,0:T(8,128)(2,1)S(1)}, u32[]{:S(2)}, u32[]{:S(2)}) %collective-permute-start.31) | collective-permute-done | bytes 524320 | tf_op jit(solution)/shard_map/ppermute | solution.py:87
  718.7 4.6 all-to-all-start.6
  724.4 21.9 %collective-permute-done.32 = bf16[2,1,128,2048]{3,2,1,0:T(8,128)(2,1)S(1)} collective-permute-done((bf16[2,1,128,2048]{3,2,1,0:T(8,128)(2,1)}, bf16[2,1,128,2048]{3,2,1,0:T(8,128)(2,1)S(1)}, u32[]{:S(2)}, u32[]{:S(2)}) %collective-permute-start.32) | collective-permute-done | bytes 1048608 | tf_op jit(solution)/shard_map/ppermute | solution.py:87
  753.3 21.7 %attend_back.1 = (bf16[2,2,128,2688]{3,2,1,0:T(8,128)(2,1)}, bf16[2,2,128,2688]{3,2,1,0:T(8,128)(2,1)}, bf16[1024,384]{1,0:T(8,128)(2,1)}, bf16[1024,512]{1,0:T(8,128)(2,1)}) custom-call(bf16[1024,2048]{1,0:T(8,128)(2,1)} %bitcast.211, bf16[256,2048]{1,0:T(8,128)(2,1)} %bitcast.222, bf16[2,1024,1024]{2,1,0:T(8,128)(2,1)} %get-tuple-element.141.refs_2_, ...), custom_call_target="tpu_custom_call" | custom-call | bytes 1000000 | tf_op jit(solution)/shard_map/attend_back/pallas_call | solution.py:483
  775.0 11.5 %all-to-all-done.6 = bf16[4,704,512]{2,1,0:T(8,128)(2,1)} async-done(((bf16[4,704,512]{2,1,0:T(8,128)(2,1)}), bf16[4,704,512]{2,1,0:T(8,128)(2,1)}, u32[]{:S(2)}, u32[]{:S(2)}) %all-to-all-start.6) | async-done | bytes 2883616 | tf_op jit(solution)/shard_map/all_to_all | solution.py:794
  786.5 5.3 collective-permute-done.34
  796.9 4.8 all-to-all-start.8
  801.8 26.5 %collective-permute-done.35 = bf16[1,2,128,2688]{3,2,1,0:T(8,128)(2,1)} collective-permute-done((bf16[1,2,128,2688]{3,2,1,0:T(8,128)(2,1)S(1)}, bf16[1,2,128,2688]{3,2,1,0:T(8,128)(2,1)}, u32[]{:S(2)}, u32[]{:S(2)}) %collective-permute-start.35) | collective-permute-done | bytes 1376288 | tf_op jit(solution)/shard_map/ppermute | solution.py:87
  834.8 10.6 assemble.3
  848.5 9.0 attend_weights.1
  857.6 21.5 %collective-permute-done.36 = bf16[1,128,2688]{2,1,0:T(8,128)(2,1)} collective-permute-done((bf16[1,128,2688]{2,1,0:T(8,128)(2,1)}, bf16[1,128,2688]{2,1,0:T(8,128)(2,1)}, u32[]{:S(2)}, u32[]{:S(2)}) %collective-permute-start.36) | collective-permute-done | bytes 688160 | tf_op jit(solution)/shard_map/ppermute | solution.py:87
  891.1 6.2 collective-permute-done.40
  926.2 16.1 %collective-permute-done.38 = bf16[1,2,128,2048]{3,2,1,0:T(8,128)(2,1)S(1)} collective-permute-done((bf16[1,2,128,2048]{3,2,1,0:T(8,128)(2,1)S(1)}, bf16[1,2,128,2048]{3,2,1,0:T(8,128)(2,1)S(1)}, u32[]{:S(2)}, u32[]{:S(2)}) %collective-permute-start.38) | collective-permute-done | bytes 1048608 | tf_op jit(solution)/shard_map/ppermute | solution.py:87
  942.8 23.7 %collective-permute-done.37 = bf16[1,2,128,2048]{3,2,1,0:T(8,128)(2,1)S(1)} collective-permute-done((bf16[1,2,128,2048]{3,2,1,0:T(8,128)(2,1)S(1)}, bf16[1,2,128,2048]{3,2,1,0:T(8,128)(2,1)S(1)}, u32[]{:S(2)}, u32[]{:S(2)}) %collective-permute-start.37) | collective-permute-done | bytes 1048608 | tf_op jit(solution)/shard_map/ppermute | solution.py:87
  978.4 10.8 assemble.4
  994.9 6.0 collective-permute-done.43
  1002.5 28.5 %collective-permute-done.44 = bf16[1,912,512]{2,1,0:T(8,128)(2,1)S(1)} collective-permute-done((bf16[1,912,512]{2,1,0:T(8,128)(2,1)S(1)}, bf16[1,912,512]{2,1,0:T(8,128)(2,1)S(1)}, u32[]{:S(2)}, u32[]{:S(2)}) %collective-permute-start.44) | collective-permute-done | bytes 933920 | tf_op jit(solution)/shard_map/ppermute | solution.py:87
  1038.2 21.2 %collective-permute-done.45 = bf16[1,128,2048]{2,1,0:T(8,128)(2,1)} collective-permute-done((bf16[1,128,2048]{2,1,0:T(8,128)(2,1)}, bf16[1,128,2048]{2,1,0:T(8,128)(2,1)}, u32[]{:S(2)}, u32[]{:S(2)}) %collective-permute-start.45) | collective-permute-done | bytes 524320 | tf_op jit(solution)/shard_map/ppermute | solution.py:87
  1107.8 16.3 %assemble.5 = f32[16,704,512]{2,1,0:T(8,128)} custom-call(s32[16]{0:T(128)S(1)} %iota.57.dest_ref, bf16[16,968,512]{2,1,0:T(8,128)(2,1)} %all-gather.27.cloned.1.call-done.refs_0_), custom_call_target="tpu_custom_call" | custom-call | bytes 36000000 | tf_op jit(solution)/shard_map/assemble/pallas_call | solution.py:665
  (491 shorter events, 360.6 us)
Async XLA Ops:
  7.3 57.4 %all-gather.15.cloned.1.call-start = ((), (), s32[]{:S(2)}) async-start(), calls=%async_computation.9 | async-start | bytes 2785280 | tf_op jit(solution)/shard_map/all_gather | solution.py:831
  8.8 26.3 %collective-permute-start = (bf16[1,256,2048]{2,1,0:T(8,128)(2,1)S(1)}, bf16[1,256,2048]{2,1,0:T(8,128)(2,1)}, u32[]{:S(2)}, u32[]{:S(2)}) collective-permute-start(bf16[1,256,2048]{2,1,0:T(8,128)(2,1)S(1)} %maximum_bitcast_fusion), channel_id=1, source_target_pairs={{0,4},{2,6},{4,0},{6,2},{1,5},{3,7},{5,1},{7,3},{8,12},{10,14},{12... | collective-permute-start | bytes 3145736 | tf_op jit(solution)/shard_map/ppermute | solution.py:87
  15.8 92.9 %all-gather.17.cloned.1.call-start = ((), (), s32[]{:S(2)}) async-start(), calls=%async_computation.10 | async-start | bytes 1966080 | tf_op jit(solution)/shard_map/all_gather | solution.py:847
  73.5 100.9 %all-gather.19.cloned.1.call-start = ((), (), s32[]{:S(2)}) async-start(), calls=%async_computation.11 | async-start | bytes 2621440 | tf_op jit(solution)/shard_map/all_gather | solution.py:859
  141.4 75.7 %all-to-all-start = ((bf16[4,704,512]{2,1,0:T(8,128)(2,1)}), bf16[4,704,512]{2,1,0:T(8,128)(2,1)S(1)}, u32[]{:S(2)}, u32[]{:S(2)}) async-start(bf16[4,704,512]{2,1,0:T(8,128)(2,1)} %dynamic-slice_bitcast_fusion.1), calls=%async_computation | async-start | bytes 5767168 | tf_op jit(solution)/shard_map/all_to_all | solution.py:794
  145.0 121.0 %all-gather.21.cloned.1.call-start = ((), (), s32[]{:S(2)}) async-start(), calls=%async_computation.12 | async-start | bytes 2621440 | tf_op jit(solution)/shard_map/all_gather | solution.py:910
  175.9 24.5 %collective-permute-start.7 = (bf16[1,2,128,2048]{3,2,1,0:T(8,128)(2,1)S(1)}, bf16[1,2,128,2048]{3,2,1,0:T(8,128)(2,1)S(1)}, u32[]{:S(2)}, u32[]{:S(2)}) collective-permute-start(bf16[1,2,128,2048]{3,2,1,0:T(8,128)(2,1)S(1)} %slice.256), channel_id=1, source_target_pairs={{0,1},{1,0},{2,3},{3,2},{4,5},{5,4},{6,7},{7,6},{8,9},{9,8},{10,11... | collective-permute-start | bytes 3145736 | tf_op jit(solution)/shard_map/ppermute | solution.py:87
  222.9 25.1 %collective-permute-start.9 = (bf16[1,1,2,128,2048]{4,3,2,1,0:T(8,128)(2,1)S(1)}, bf16[1,1,2,128,2048]{4,3,2,1,0:T(8,128)(2,1)S(1)}, u32[]{:S(2)}, u32[]{:S(2)}) collective-permute-start(bf16[1,1,2,128,2048]{4,3,2,1,0:T(8,128)(2,1)S(1)} %get-tuple-element.258), channel_id=1, source_target_pairs={{0,4},{2,6},{4,0},{6,2},{1,5},{3,7},{5,1},{7,3},{8,12},{10,14},{12... | collective-permute-start | bytes 3145736 | tf_op jit(solution)/shard_map/ppermute | solution.py:87
  224.5 26.5 %collective-permute-start.11 = (bf16[1,1,2,128,2048]{4,3,2,1,0:T(8,128)(2,1)S(1)}, bf16[1,1,2,128,2048]{4,3,2,1,0:T(8,128)(2,1)S(1)}, u32[]{:S(2)}, u32[]{:S(2)}) collective-permute-start(bf16[1,1,2,128,2048]{4,3,2,1,0:T(8,128)(2,1)S(1)} %get-tuple-element.257), channel_id=1, source_target_pairs={{0,1},{1,0},{2,3},{3,2},{4,5},{5,4},{6,7},{7,6},{8,9},{9,8},{10,11... | collective-permute-start | bytes 3145736 | tf_op jit(solution)/shard_map/ppermute | solution.py:87
  249.5 47.1 %collective-permute-start.10 = (bf16[2,1,2,128,2048]{4,3,2,1,0:T(8,128)(2,1)}, bf16[2,1,2,128,2048]{4,3,2,1,0:T(8,128)(2,1)}, u32[]{:S(2)}, u32[]{:S(2)}) collective-permute-start(bf16[2,1,2,128,2048]{4,3,2,1,0:T(8,128)(2,1)} %pad_maximum_fusion.7), channel_id=1, source_target_pairs={{0,1},{1,0},{2,3},{3,2},{4,5},{5,4},{6,7},{7,6},{8,9},{9,8},{10,11... | collective-permute-start | bytes 6291464 | tf_op jit(solution)/shard_map/ppermute | solution.py:87
  252.5 47.3 %collective-permute-start.12 = (bf16[1,2,2,128,2048]{4,3,2,1,0:T(8,128)(2,1)}, bf16[1,2,2,128,2048]{4,3,2,1,0:T(8,128)(2,1)}, u32[]{:S(2)}, u32[]{:S(2)}) collective-permute-start(bf16[1,2,2,128,2048]{4,3,2,1,0:T(8,128)(2,1)} %pad_maximum_fusion.8), channel_id=1, source_target_pairs={{0,4},{2,6},{4,0},{6,2},{1,5},{3,7},{5,1},{7,3},{8,12},{10,14},{12... | collective-permute-start | bytes 6291464 | tf_op jit(solution)/shard_map/ppermute | solution.py:87
  266.1 76.1 %all-to-all-start.1 = ((bf16[4,704,512]{2,1,0:T(8,128)(2,1)}), bf16[4,704,512]{2,1,0:T(8,128)(2,1)S(1)}, u32[]{:S(2)}, u32[]{:S(2)}) async-start(bf16[4,704,512]{2,1,0:T(8,128)(2,1)} %dynamic-slice_bitcast_fusion), calls=%async_computation.1 | async-start | bytes 5767168 | tf_op jit(solution)/shard_map/all_to_all | solution.py:794
  303.4 23.4 %collective-permute-start.13 = (bf16[1,1,2,128,2048]{4,3,2,1,0:T(8,128)(2,1)S(1)}, bf16[1,1,2,128,2048]{4,3,2,1,0:T(8,128)(2,1)S(1)}, u32[]{:S(2)}, u32[]{:S(2)}) collective-permute-start(bf16[1,1,2,128,2048]{4,3,2,1,0:T(8,128)(2,1)S(1)} %get-tuple-element.256), channel_id=1, source_target_pairs={{0,4},{2,6},{4,0},{6,2},{1,5},{3,7},{5,1},{7,3},{8,12},{10,14},{12... | collective-permute-start | bytes 3145736 | tf_op jit(solution)/shard_map/ppermute | solution.py:87
  304.9 25.0 %collective-permute-start.16 = (bf16[1,1,2,128,2048]{4,3,2,1,0:T(8,128)(2,1)S(1)}, bf16[1,1,2,128,2048]{4,3,2,1,0:T(8,128)(2,1)S(1)}, u32[]{:S(2)}, u32[]{:S(2)}) collective-permute-start(bf16[1,1,2,128,2048]{4,3,2,1,0:T(8,128)(2,1)S(1)} %get-tuple-element.255), channel_id=1, source_target_pairs={{0,1},{1,0},{2,3},{3,2},{4,5},{5,4},{6,7},{7,6},{8,9},{9,8},{10,11... | collective-permute-start | bytes 3145736 | tf_op jit(solution)/shard_map/ppermute | solution.py:87
  328.5 45.2 %collective-permute-start.14 = (bf16[2,1,2,128,2048]{4,3,2,1,0:T(8,128)(2,1)}, bf16[2,1,2,128,2048]{4,3,2,1,0:T(8,128)(2,1)}, u32[]{:S(2)}, u32[]{:S(2)}) collective-permute-start(bf16[2,1,2,128,2048]{4,3,2,1,0:T(8,128)(2,1)} %pad_maximum_fusion.9), channel_id=1, source_target_pairs={{0,1},{1,0},{2,3},{3,2},{4,5},{5,4},{6,7},{7,6},{8,9},{9,8},{10,11... | collective-permute-start | bytes 6291464 | tf_op jit(solution)/shard_map/ppermute | solution.py:87
  332.4 48.6 %collective-permute-start.17 = (bf16[1,2,2,128,2048]{4,3,2,1,0:T(8,128)(2,1)}, bf16[1,2,2,128,2048]{4,3,2,1,0:T(8,128)(2,1)}, u32[]{:S(2)}, u32[]{:S(2)}) collective-permute-start(bf16[1,2,2,128,2048]{4,3,2,1,0:T(8,128)(2,1)} %pad_maximum_fusion.10), channel_id=1, source_target_pairs={{0,4},{2,6},{4,0},{6,2},{1,5},{3,7},{5,1},{7,3},{8,12},{10,14},{12... | collective-permute-start | bytes 6291464 | tf_op jit(solution)/shard_map/ppermute | solution.py:87
  345.3 31.8 %all-to-all-start.2 = ((bf16[4,3,88,512]{3,2,1,0:T(8,128)(2,1)}), bf16[4,3,88,512]{3,2,1,0:T(8,128)(2,1)}, u32[]{:S(2)}, u32[]{:S(2)}) async-start(bf16[4,3,88,512]{3,2,1,0:T(8,128)(2,1)} %copy.147), calls=%async_computation.2 | async-start | bytes 2162688 | tf_op jit(solution)/shard_map/all_to_all | solution.py:794
  353.3 37.0 %collective-permute-start.19 = (bf16[2,2,2,128,2048]{4,3,2,1,0:T(8,128)(2,1)}, bf16[2,2,2,128,2048]{4,3,2,1,0:T(8,128)(2,1)}, u32[]{:S(2)}, u32[]{:S(2)}) collective-permute-start(bf16[2,2,2,128,2048]{4,3,2,1,0:T(8,128)(2,1)} %constant_dynamic-update-slice_fusion.6.refs_6_), channel_id=1, source_target_pairs={{0,2},{2,0},{4,6},{6,4},{1,3},{3,1},{5,7},{7,5},{8,10},{10,8},{12,... | collective-permute-start | bytes 12582920 | tf_op jit(solution)/shard_map/ppermute | solution.py:87
  353.3 37.0 %collective-permute-start.20 = (bf16[2,2,2,128,2048]{4,3,2,1,0:T(8,128)(2,1)}, bf16[2,2,2,128,2048]{4,3,2,1,0:T(8,128)(2,1)}, u32[]{:S(2)}, u32[]{:S(2)}) collective-permute-start(bf16[2,2,2,128,2048]{4,3,2,1,0:T(8,128)(2,1)} %constant_dynamic-update-slice_fusion.8.refs_8_), channel_id=1, source_target_pairs={{0,2},{2,0},{4,6},{6,4},{1,3},{3,1},{5,7},{7,5},{8,10},{10,8},{12,... | collective-permute-start | bytes 12582920 | tf_op jit(solution)/shard_map/ppermute | solution.py:87
  377.1 69.8 %all-to-all-start.3 = ((bf16[4,704,512]{2,1,0:T(8,128)(2,1)}), bf16[4,704,512]{2,1,0:T(8,128)(2,1)S(1)}, u32[]{:S(2)}, u32[]{:S(2)}) async-start(bf16[4,704,512]{2,1,0:T(8,128)(2,1)} %constant_dynamic-slice_fusion), calls=%async_computation.3 | async-start | bytes 5767168 | tf_op jit(solution)/shard_map/all_to_all | solution.py:794
  530.0 62.5 %collective-permute-start.26 = (bf16[1,2,2,128,2176]{4,3,2,1,0:T(8,128)(2,1)}, bf16[1,2,2,128,2176]{4,3,2,1,0:T(8,128)(2,1)}, u32[]{:S(2)}, u32[]{:S(2)}) collective-permute-start(bf16[1,2,2,128,2176]{4,3,2,1,0:T(8,128)(2,1)} %slice.329), channel_id=1, source_target_pairs={{0,4},{2,6},{4,0},{6,2},{1,5},{3,7},{5,1},{7,3},{8,12},{10,14},{12... | collective-permute-start | bytes 6684680 | tf_op jit(solution)/shard_map/ppermute | solution.py:87
  534.5 62.0 %collective-permute-start.24 = (bf16[1,2,2,128,2176]{4,3,2,1,0:T(8,128)(2,1)}, bf16[1,2,2,128,2176]{4,3,2,1,0:T(8,128)(2,1)}, u32[]{:S(2)}, u32[]{:S(2)}) collective-permute-start(bf16[1,2,2,128,2176]{4,3,2,1,0:T(8,128)(2,1)} %slice.327), channel_id=1, source_target_pairs={{0,1},{1,0},{2,3},{3,2},{4,5},{5,4},{6,7},{7,6},{8,9},{9,8},{10,11... | collective-permute-start | bytes 6684680 | tf_op jit(solution)/shard_map/ppermute | solution.py:87
  564.6 63.0 %collective-permute-start.29 = (bf16[2,2,2,128,2048]{4,3,2,1,0:T(8,128)(2,1)}, bf16[2,2,2,128,2048]{4,3,2,1,0:T(8,128)(2,1)}, u32[]{:S(2)}, u32[]{:S(2)}) collective-permute-start(bf16[2,2,2,128,2048]{4,3,2,1,0:T(8,128)(2,1)} %get-tuple-element.130), channel_id=1, source_target_pairs={{0,2},{2,0},{4,6},{6,4},{1,3},{3,1},{5,7},{7,5},{8,10},{10,8},{12,... | collective-permute-start | bytes 12582920 | tf_op jit(solution)/shard_map/ppermute | solution.py:87
  564.6 71.1 %all-to-all-start.4 = ((bf16[4,704,512]{2,1,0:T(8,128)(2,1)}), bf16[4,704,512]{2,1,0:T(8,128)(2,1)}, u32[]{:S(2)}, u32[]{:S(2)}) async-start(bf16[4,704,512]{2,1,0:T(8,128)(2,1)} %copy-done.13), calls=%async_computation.4 | async-start | bytes 5767168 | tf_op jit(solution)/shard_map/all_to_all | solution.py:794
  592.0 52.6 %collective-permute-start.23 = (bf16[2,2,2,128,2048]{4,3,2,1,0:T(8,128)(2,1)}, bf16[2,2,2,128,2048]{4,3,2,1,0:T(8,128)(2,1)}, u32[]{:S(2)}, u32[]{:S(2)}) collective-permute-start(bf16[2,2,2,128,2048]{4,3,2,1,0:T(8,128)(2,1)} %get-tuple-element.128), channel_id=1, source_target_pairs={{0,2},{2,0},{4,6},{6,4},{1,3},{3,1},{5,7},{7,5},{8,10},{10,8},{12,... | collective-permute-start | bytes 12582920 | tf_op jit(solution)/shard_map/ppermute | solution.py:87
  595.5 26.5 %collective-permute-start.27 = (bf16[1,2,128,2176]{3,2,1,0:T(8,128)(2,1)S(1)}, bf16[1,2,128,2176]{3,2,1,0:T(8,128)(2,1)S(1)}, u32[]{:S(2)}, u32[]{:S(2)}) collective-permute-start(bf16[1,2,128,2176]{3,2,1,0:T(8,128)(2,1)S(1)} %slice.271), channel_id=1, source_target_pairs={{0,1},{1,0},{2,3},{3,2},{4,5},{5,4},{6,7},{7,6},{8,9},{9,8},{10,11... | collective-permute-start | bytes 3342344 | tf_op jit(solution)/shard_map/ppermute | solution.py:87
  599.5 26.3 %collective-permute-start.25 = (bf16[1,2,128,2176]{3,2,1,0:T(8,128)(2,1)S(1)}, bf16[1,2,128,2176]{3,2,1,0:T(8,128)(2,1)S(1)}, u32[]{:S(2)}, u32[]{:S(2)}) collective-permute-start(bf16[1,2,128,2176]{3,2,1,0:T(8,128)(2,1)S(1)} %slice.267), channel_id=1, source_target_pairs={{0,4},{2,6},{4,0},{6,2},{1,5},{3,7},{5,1},{7,3},{8,12},{10,14},{12... | collective-permute-start | bytes 3342344 | tf_op jit(solution)/shard_map/ppermute | solution.py:87
  635.7 65.7 %all-to-all-start.5 = ((bf16[4,128,2176]{2,1,0:T(8,128)(2,1)}), bf16[4,128,2176]{2,1,0:T(8,128)(2,1)}, u32[]{:S(2)}, u32[]{:S(2)}) async-start(bf16[4,128,2176]{2,1,0:T(8,128)(2,1)} %pad_maximum_fusion.5), calls=%async_computation.5 | async-start | bytes 4456448 | tf_op jit(solution)/shard_map/all_to_all | solution.py:794
  640.2 190.2 %all-gather.23.cloned.1.call-start = ((), (), s32[]{:S(2)}) async-start(), calls=%async_computation.13 | async-start | bytes 14417920 | tf_op jit(solution)/shard_map/all_gather | solution.py:1004
  643.6 47.6 %collective-permute-start.30 = (bf16[1,2,2,128,2048]{4,3,2,1,0:T(8,128)(2,1)}, bf16[1,2,2,128,2048]{4,3,2,1,0:T(8,128)(2,1)}, u32[]{:S(2)}, u32[]{:S(2)}) collective-permute-start(bf16[1,2,2,128,2048]{4,3,2,1,0:T(8,128)(2,1)} %slice.275), channel_id=1, source_target_pairs={{0,4},{2,6},{4,0},{6,2},{1,5},{3,7},{5,1},{7,3},{8,12},{10,14},{12... | collective-permute-start | bytes 6291464 | tf_op jit(solution)/shard_map/ppermute | solution.py:87
  650.4 47.2 %collective-permute-start.28 = (bf16[1,2,2,128,2048]{4,3,2,1,0:T(8,128)(2,1)}, bf16[1,2,2,128,2048]{4,3,2,1,0:T(8,128)(2,1)}, u32[]{:S(2)}, u32[]{:S(2)}) collective-permute-start(bf16[1,2,2,128,2048]{4,3,2,1,0:T(8,128)(2,1)} %slice.273), channel_id=1, source_target_pairs={{0,1},{1,0},{2,3},{3,2},{4,5},{5,4},{6,7},{7,6},{8,9},{9,8},{10,11... | collective-permute-start | bytes 6291464 | tf_op jit(solution)/shard_map/ppermute | solution.py:87
  718.7 67.7 %all-to-all-start.6 = ((bf16[4,704,512]{2,1,0:T(8,128)(2,1)}), bf16[4,704,512]{2,1,0:T(8,128)(2,1)}, u32[]{:S(2)}, u32[]{:S(2)}) async-start(bf16[4,704,512]{2,1,0:T(8,128)(2,1)} %weight_grads.4), calls=%async_computation.6 | async-start | bytes 5767168 | tf_op jit(solution)/shard_map/all_to_all | solution.py:794
  723.3 250.6 %all-gather.25.cloned.1.call-start = ((), (), s32[]{:S(2)}) async-start(), calls=%async_computation.14 | async-start | bytes 14417920 | tf_op jit(solution)/shard_map/all_gather | solution.py:1024
  723.4 22.9 %collective-permute-start.32 = (bf16[2,1,128,2048]{3,2,1,0:T(8,128)(2,1)}, bf16[2,1,128,2048]{3,2,1,0:T(8,128)(2,1)S(1)}, u32[]{:S(2)}, u32[]{:S(2)}) collective-permute-start(bf16[2,1,128,2048]{3,2,1,0:T(8,128)(2,1)} %pad_maximum_fusion.16), channel_id=1, source_target_pairs={{0,1},{1,0},{2,3},{3,2},{4,5},{5,4},{6,7},{7,6},{8,9},{9,8},{10,11... | collective-permute-start | bytes 3145736 | tf_op jit(solution)/shard_map/ppermute | solution.py:87
  795.9 32.4 %collective-permute-start.35 = (bf16[1,2,128,2688]{3,2,1,0:T(8,128)(2,1)S(1)}, bf16[1,2,128,2688]{3,2,1,0:T(8,128)(2,1)}, u32[]{:S(2)}, u32[]{:S(2)}) collective-permute-start(bf16[1,2,128,2688]{3,2,1,0:T(8,128)(2,1)S(1)} %slice.278), channel_id=1, source_target_pairs={{0,1},{1,0},{2,3},{3,2},{4,5},{5,4},{6,7},{7,6},{8,9},{9,8},{10,11... | collective-permute-start | bytes 4128776 | tf_op jit(solution)/shard_map/ppermute | solution.py:87
  796.9 109.3 %all-to-all-start.8 = ((bf16[4,968,512]{2,1,0:T(8,128)(2,1)}), bf16[4,968,512]{2,1,0:T(8,128)(2,1)}, u32[]{:S(2)}, u32[]{:S(2)}) async-start(bf16[4,968,512]{2,1,0:T(8,128)(2,1)} %weight_grads.5), calls=%async_computation.8 | async-start | bytes 7929856 | tf_op jit(solution)/shard_map/all_to_all | solution.py:794
  801.7 293.2 %all-gather.27.cloned.1.call-start = ((), (), s32[]{:S(2)}) async-start(), calls=%async_computation.15 | async-start | bytes 19824640 | tf_op jit(solution)/shard_map/all_gather | solution.py:1061
  846.3 32.8 %collective-permute-start.36 = (bf16[1,128,2688]{2,1,0:T(8,128)(2,1)}, bf16[1,128,2688]{2,1,0:T(8,128)(2,1)}, u32[]{:S(2)}, u32[]{:S(2)}) collective-permute-start(bf16[1,128,2688]{2,1,0:T(8,128)(2,1)} %slice.280), channel_id=1, source_target_pairs={{0,4},{2,6},{4,0},{6,2},{1,5},{3,7},{5,1},{7,3},{8,12},{10,14},{12... | collective-permute-start | bytes 2064392 | tf_op jit(solution)/shard_map/ppermute | solution.py:87
  916.2 26.1 %collective-permute-start.38 = (bf16[1,2,128,2048]{3,2,1,0:T(8,128)(2,1)S(1)}, bf16[1,2,128,2048]{3,2,1,0:T(8,128)(2,1)S(1)}, u32[]{:S(2)}, u32[]{:S(2)}) collective-permute-start(bf16[1,2,128,2048]{3,2,1,0:T(8,128)(2,1)S(1)} %slice.284), channel_id=1, source_target_pairs={{0,1},{1,0},{2,3},{3,2},{4,5},{5,4},{6,7},{7,6},{8,9},{9,8},{10,11... | collective-permute-start | bytes 3145736 | tf_op jit(solution)/shard_map/ppermute | solution.py:87
  918.6 47.9 %collective-permute-start.37 = (bf16[1,2,128,2048]{3,2,1,0:T(8,128)(2,1)S(1)}, bf16[1,2,128,2048]{3,2,1,0:T(8,128)(2,1)S(1)}, u32[]{:S(2)}, u32[]{:S(2)}) collective-permute-start(bf16[1,2,128,2048]{3,2,1,0:T(8,128)(2,1)S(1)} %slice.282), channel_id=1, source_target_pairs={{0,4},{2,6},{4,0},{6,2},{1,5},{3,7},{5,1},{7,3},{8,12},{10,14},{12... | collective-permute-start | bytes 3145736 | tf_op jit(solution)/shard_map/ppermute | solution.py:87
  921.5 45.6 %collective-permute-start.42 = (bf16[2,912,512]{2,1,0:T(8,128)(2,1)S(1)}, bf16[2,912,512]{2,1,0:T(8,128)(2,1)S(1)}, u32[]{:S(2)}, u32[]{:S(2)}) collective-permute-start(bf16[2,912,512]{2,1,0:T(8,128)(2,1)S(1)} %dynamic-slice_bitcast_fusion.2), channel_id=1, source_target_pairs={{0,8},{8,0},{16,24},{24,16},{1,9},{9,1},{17,25},{25,17},{2,10},{10... | collective-permute-start | bytes 5603336 | tf_op jit(solution)/shard_map/ppermute | solution.py:87
  924.8 66.9 %collective-permute-start.47 = (bf16[1,1,128,2048]{3,2,1,0:T(8,128)(2,1)}, bf16[1,1,128,2048]{3,2,1,0:T(8,128)(2,1)}, u32[]{:S(2)}, u32[]{:S(2)}) collective-permute-start(bf16[1,1,128,2048]{3,2,1,0:T(8,128)(2,1)} %fusion.29), channel_id=1, source_target_pairs={{0,1},{1,0},{2,3},{3,2},{4,5},{5,4},{6,7},{7,6},{8,9},{9,8},{10,11... | collective-permute-start | bytes 1572872 | tf_op jit(solution)/shard_map/ppermute | solution.py:87
  970.6 30.3 %collective-permute-start.43 = (bf16[2,128,2048]{2,1,0:T(8,128)(2,1)}, bf16[2,128,2048]{2,1,0:T(8,128)(2,1)}, u32[]{:S(2)}, u32[]{:S(2)}) collective-permute-start(bf16[2,128,2048]{2,1,0:T(8,128)(2,1)} %dynamic-slice_bitcast_fusion.3), channel_id=1, source_target_pairs={{0,8},{8,0},{16,24},{24,16},{1,9},{9,1},{17,25},{25,17},{2,10},{10... | collective-permute-start | bytes 3145736 | tf_op jit(solution)/shard_map/ppermute | solution.py:87
  989.4 41.6 %collective-permute-start.44 = (bf16[1,912,512]{2,1,0:T(8,128)(2,1)S(1)}, bf16[1,912,512]{2,1,0:T(8,128)(2,1)S(1)}, u32[]{:S(2)}, u32[]{:S(2)}) collective-permute-start(bf16[1,912,512]{2,1,0:T(8,128)(2,1)S(1)} %dynamic-slice_convert_fusion), channel_id=1, source_target_pairs={{0,16},{8,24},{16,0},{24,8},{1,17},{9,25},{17,1},{25,9},{2,18},{10... | collective-permute-start | bytes 2801672 | tf_op jit(solution)/shard_map/ppermute | solution.py:87
  1031.3 30.9 %collective-permute-start.49 = (bf16[912,512]{1,0:T(8,128)(2,1)S(1)}, bf16[912,512]{1,0:T(8,128)(2,1)}, u32[]{:S(2)}, u32[]{:S(2)}) collective-permute-start(bf16[912,512]{1,0:T(8,128)(2,1)S(1)} %add_bitcast_fusion), channel_id=1, source_target_pairs={{0,4},{2,6},{4,0},{6,2},{1,5},{3,7},{5,1},{7,3},{8,12},{10,14},{12... | collective-permute-start | bytes 2801672 | tf_op jit(solution)/shard_map/ppermute | solution.py:87
  1032.0 35.3 %collective-permute-start.53 = (bf16[912,512]{1,0:T(8,128)(2,1)S(1)}, bf16[912,512]{1,0:T(8,128)(2,1)}, u32[]{:S(2)}, u32[]{:S(2)}) collective-permute-start(bf16[912,512]{1,0:T(8,128)(2,1)S(1)} %add_bitcast_fusion), channel_id=1, source_target_pairs={{0,2},{2,0},{4,6},{6,4},{1,3},{3,1},{5,7},{7,5},{8,10},{10,8},{12,... | collective-permute-start | bytes 2801672 | tf_op jit(solution)/shard_map/ppermute | solution.py:87
  1032.8 26.5 %collective-permute-start.45 = (bf16[1,128,2048]{2,1,0:T(8,128)(2,1)}, bf16[1,128,2048]{2,1,0:T(8,128)(2,1)}, u32[]{:S(2)}, u32[]{:S(2)}) collective-permute-start(bf16[1,128,2048]{2,1,0:T(8,128)(2,1)} %dynamic-slice_convert_fusion.1), channel_id=1, source_target_pairs={{0,16},{8,24},{16,0},{24,8},{1,17},{9,25},{17,1},{25,9},{2,18},{10... | collective-permute-start | bytes 1572872 | tf_op jit(solution)/shard_map/ppermute | solution.py:87
  1060.6 25.5 %collective-permute-start.46 = (bf16[1,1,128,2048]{3,2,1,0:T(8,128)(2,1)S(1)}, bf16[1,1,128,2048]{3,2,1,0:T(8,128)(2,1)S(1)}, u32[]{:S(2)}, u32[]{:S(2)}) collective-permute-start(bf16[1,1,128,2048]{3,2,1,0:T(8,128)(2,1)S(1)} %fusion.28), channel_id=1, source_target_pairs={{0,1},{1,0},{2,3},{3,2},{4,5},{5,4},{6,7},{7,6},{8,9},{9,8},{10,11... | collective-permute-start | bytes 1572872 | tf_op jit(solution)/shard_map/ppermute | solution.py:87
  (100 other events, 1161.7 us)
Sparse Core Ops, SparseCore 0:
  16.0 48.6 all-gather.14
  73.6 35.0 all-gather.16
  110.8 63.5 all-gather.18
  221.4 44.6 all-gather.20
  718.8 75.9 all-gather.22
  796.2 90.8 all-gather.24
  906.4 123.8 all-gather.26
